TPU v7x, 32 devices: a whole 2x2x4 slice. The times are simulated.
32 devices in a mesh: lat: 4 (over y, x), lon: 8 (over z, core).
Axes of the slice: x: 2, y: 2, z: 4, core: 2. Of those that a mesh axis runs over, the one named last changes fastest.
Arguments:
- air_mass: float32 [4, 32, 11520], P(None, 'lat', 'lon'), may hold values from 0.5 to 2
- tracer_mass: float32 [4, 4, 32, 11520], P(None, None, 'lat', 'lon'), may hold values from -6 to 6
- zonal_frac: float32 [4, 32, 11520], P(None, 'lat', 'lon'), may hold values from 0.05 to 0.95
- merid_courant: float32 [4, 32, 11520], P(None, 'lat', 'lon'), may hold values from -0.45 to 0.45
- zonal_shift: int32 [4, 32], P(None, 'lat'), may hold values from -5759 to 5759, as said below
Outputs:
- air_out: float32 [4, 32, 11520], P(None, 'lat', 'lon')
- tracer_out: float32 [4, 4, 32, 11520], P(None, None, 'lat', 'lon')
Inputs may be any that keep to these rules, and one draw needn't show every extreme that they name: `zonal_shift`: row j lies (j + 1/2) / 5760 of a half circle from the pole; its whole-cell shifts may carry it across many longitude devices, in either direction.
All inputs are finite; a program needn't handle non-finite values.
Results may differ from a plain program's by a relative error of at most 0.0003.
Values sent between devices are 32-bit elements; how exact they have to be, the bound alone decides.
A program may use at most 64 MiB of HBM per device.

v0:
```python
import jax
import jax.numpy as jnp
from jax import lax
from jax.sharding import PartitionSpec as P

ITERS = 2


def from_behind(array, axis, by):
    count = lax.axis_size(axis)
    return lax.ppermute(array, axis, [(i, (i + by) % count) for i in range(count)])


def padded_2(block, sides, width, periodic):
    for axis, dim in sides:
        count = lax.axis_size(axis)
        forward = [(i, i + 1) for i in range(count - 1)]
        if periodic:
            forward.append((count - 1, 0))
        backward = [(target, source) for source, target in forward]
        low = lax.ppermute(
            lax.slice_in_dim(block, block.shape[dim] - width, None, axis=dim), axis, forward
        )
        high = lax.ppermute(lax.slice_in_dim(block, 0, width, axis=dim), axis, backward)
        block = jnp.concatenate([low, block, high], axis=dim)
    return block


def right_amount(centre, left_edge, right_edge, fraction):
    slope = right_edge - left_edge
    curve = 6.0 * centre - 3.0 * (left_edge + right_edge)
    return fraction * (
        right_edge - 0.5 * fraction * (slope - (1.0 - fraction * (2.0 / 3.0)) * curve)
    )


def left_amount(centre, left_edge, right_edge, fraction):
    slope = right_edge - left_edge
    curve = 6.0 * centre - 3.0 * (left_edge + right_edge)
    return fraction * (
        left_edge + 0.5 * fraction * (slope + (1.0 - fraction * (2.0 / 3.0)) * curve)
    )


def zonal_update(padded, padded_frac):
    faces = (
        7.0 * (padded[..., 1:-2] + padded[..., 2:-1]) - (padded[..., :-3] + padded[..., 3:])
    ) / 12.0
    cells = padded.shape[-1] - 6
    fluxes = right_amount(
        padded[..., 2 : cells + 3],
        faces[..., 0 : cells + 1],
        faces[..., 1 : cells + 2],
        padded_frac[..., 3 : cells + 4],
    )
    return padded[..., 3 : cells + 3] + fluxes[..., :cells] - fluxes[..., 1:]


def merid_update(padded, padded_courant):
    faces = (
        7.0 * (padded[..., 1:-2, :] + padded[..., 2:-1, :])
        - (padded[..., :-3, :] + padded[..., 3:, :])
    ) / 12.0
    cells = padded.shape[-2] - 6
    courant = padded_courant[..., 3 : cells + 4, :]
    northward = jnp.maximum(courant, 0.0)
    southward = jnp.maximum(-courant, 0.0)
    fluxes = right_amount(
        padded[..., 2 : cells + 3, :],
        faces[..., 0 : cells + 1, :],
        faces[..., 1 : cells + 2, :],
        northward,
    )
    fluxes = fluxes - left_amount(
        padded[..., 3 : cells + 4, :],
        faces[..., 1 : cells + 2, :],
        faces[..., 2 : cells + 3, :],
        southward,
    )
    return padded[..., 3 : cells + 3, :] + fluxes[..., :cells, :] - fluxes[..., 1:, :]


def roll_rows(values, amounts, span):
    result = values
    for bit in range(span.bit_length()):
        rolled = jnp.roll(result, 1 << bit, axis=-1)
        picked = amounts >> bit & 1 == 1
        result = jnp.where(picked[None, ..., None], rolled, result)
    return result


def zonal_blocks(fields, zonal_frac, device_steps, within):
    width = fields.shape[3]
    moved = fields
    bit_count = lax.axis_size("lon").bit_length() - 1
    for bit in range(bit_count):
        arrived = from_behind(moved, "lon", 1 << bit)
        chosen = device_steps >> bit & 1 == 1
        moved = jnp.where(chosen[None, :, :, None], arrived, moved)
    carried = from_behind(moved, "lon", 1)
    joined = jnp.concatenate([carried, moved], axis=3)
    aligned = roll_rows(joined, within, width - 1)[..., width:]
    stacked = jnp.concatenate([aligned, zonal_frac[None]], axis=0)
    padded = padded_2(stacked, (("lon", 3),), 3, True)
    return zonal_update(padded[:-1], padded[-1])


def local(air_mass, tracer_mass, zonal_frac, merid_courant, zonal_shift):
    fields = jnp.concatenate([air_mass[None], tracer_mass], axis=0)
    levels, band, width = air_mass.shape
    full_width = width * lax.axis_size("lon")
    global_row = lax.axis_index("lat") * band + jnp.arange(band, dtype=jnp.int32)
    courant = jnp.where(
        global_row[None, :, None] == 0, jnp.zeros_like(merid_courant), merid_courant
    )
    wrapped = jnp.mod(zonal_shift, full_width)
    device_steps = wrapped // width
    within = wrapped - device_steps * width
    for step in range(ITERS):
        fields = zonal_blocks(fields, zonal_frac, device_steps, within)
        stacked = jnp.concatenate([fields, courant[None]], axis=0)
        padded = padded_2(stacked, (("lat", 2),), 3, False)
        fields = merid_update(padded[:-1], padded[-1])
    return (fields[0], fields[1:])


def solution(mesh):
    return jax.shard_map(
        local,
        mesh=mesh,
        in_specs=(
            P(None, "lat", "lon"),
            P(None, None, "lat", "lon"),
            P(None, "lat", "lon"),
            P(None, "lat", "lon"),
            P(None, "lat"),
        ),
        out_specs=(P(None, "lat", "lon"), P(None, None, "lat", "lon")),
        check_vma=False,
    )
```

profile of v0, /device:TPU:0, one launch (start us, length us, event | category | flops | bytes accessed | tf_op | source)
XLA Modules:
  0.0 289.1 jit_solution(9106505579759560052)
XLA Ops:
  0.7 1.3 pad_maximum_fusion.16
  2.5 15.8 %collective-permute-done = f32[5,4,8,1440]{3,2,1,0:T(8,128)S(1)} collective-permute-done((f32[5,4,8,1440]{3,2,1,0:T(8,128)S(1)}, f32[5,4,8,1440]{3,2,1,0:T(8,128)S(1)}, u32[]{:S(2)}, u32[]{:S(2)}) %collective-permute-start) | collective-permute-done | bytes 921632 | tf_op jit(solution)/shard_map/ppermute | solution.py:11
  18.8 23.1 %collective-permute-done.1 = f32[5,4,8,1440]{3,2,1,0:T(8,128)S(1)} collective-permute-done((f32[5,4,8,1440]{3,2,1,0:T(8,128)S(1)}, f32[5,4,8,1440]{3,2,1,0:T(8,128)S(1)}, u32[]{:S(2)}, u32[]{:S(2)}) %collective-permute-start.1) | collective-permute-done | bytes 921632 | tf_op jit(solution)/shard_map/ppermute | solution.py:11
  43.1 41.8 %collective-permute-done.2 = f32[5,4,8,1440]{3,2,1,0:T(8,128)S(1)} collective-permute-done((f32[5,4,8,1440]{3,2,1,0:T(8,128)S(1)}, f32[5,4,8,1440]{3,2,1,0:T(8,128)S(1)}, u32[]{:S(2)}, u32[]{:S(2)}) %collective-permute-start.2) | collective-permute-done | bytes 921632 | tf_op jit(solution)/shard_map/ppermute | solution.py:11
  85.3 15.1 %collective-permute-done.3 = f32[5,4,8,1440]{3,2,1,0:T(8,128)S(1)} collective-permute-done((f32[5,4,8,1440]{3,2,1,0:T(8,128)S(1)}, f32[5,4,8,1440]{3,2,1,0:T(8,128)S(1)}, u32[]{:S(2)}, u32[]{:S(2)}) %collective-permute-start.3) | collective-permute-done | bytes 921632 | tf_op jit(solution)/shard_map/ppermute | solution.py:11
  108.5 3.5 %collective-permute-start.5 = (f32[6,4,8,3]{3,2,1,0:T(8,128)S(1)}, f32[6,4,8,3]{3,2,1,0:T(8,128)S(1)}, u32[]{:S(2)}, u32[]{:S(2)}) collective-permute-start(f32[6,4,8,3]{3,2,1,0:T(8,128)S(1)} %get-tuple-element.17), channel_id=1, source_target_pairs={{1,0},{2,1},{3,2},{4,3},{5,4},{6,5},{7,6},{0,7},{9,8},{10,9},{11,1... | collective-permute-start | bytes 6920 | tf_op jit(solution)/shard_map/ppermute | solution.py:24
  114.3 1.7 concatenate.154
  118.6 2.9 %collective-permute-start.6 = (f32[6,4,3,1440]{3,0,2,1:T(8,128)S(1)}, f32[6,4,3,1440]{3,0,2,1:T(8,128)S(1)}, u32[]{:S(2)}, u32[]{:S(2)}) collective-permute-start(f32[6,4,3,1440]{3,0,2,1:T(8,128)S(1)} %copy.23), channel_id=1, source_target_pairs={{0,8},{8,16},{16,24},{1,9},{9,17},{17,25},{2,10},{10,18},{18,26},{... | collective-permute-start | bytes 1244168 | tf_op jit(solution)/shard_map/ppermute | solution.py:21
  121.8 1.5 collective-permute-start.7
  123.3 6.8 %collective-permute-done.6 = f32[6,4,3,1440]{3,0,2,1:T(8,128)S(1)} collective-permute-done((f32[6,4,3,1440]{3,0,2,1:T(8,128)S(1)}, f32[6,4,3,1440]{3,0,2,1:T(8,128)S(1)}, u32[]{:S(2)}, u32[]{:S(2)}) %collective-permute-start.6) | collective-permute-done | bytes 414752 | tf_op jit(solution)/shard_map/ppermute | solution.py:21
  130.4 14.3 %collective-permute-done.7 = f32[6,4,3,1440]{3,0,2,1:T(8,128)S(1)} collective-permute-done((f32[6,4,3,1440]{3,0,2,1:T(8,128)S(1)}, f32[6,4,3,1440]{3,0,2,1:T(8,128)S(1)}, u32[]{:S(2)}, u32[]{:S(2)}) %collective-permute-start.7) | collective-permute-done | bytes 414752 | tf_op jit(solution)/shard_map/ppermute | solution.py:24
  147.1 1.8 fusion.30
  149.2 15.3 %collective-permute-done.8 = f32[5,4,8,1440]{3,2,1,0:T(8,128)S(1)} collective-permute-done((f32[5,4,8,1440]{3,2,1,0:T(8,128)S(1)}, f32[5,4,8,1440]{3,2,1,0:T(8,128)S(1)}, u32[]{:S(2)}, u32[]{:S(2)}) %collective-permute-start.8) | collective-permute-done | bytes 921632 | tf_op jit(solution)/shard_map/ppermute | solution.py:11
  164.8 21.7 %collective-permute-done.9 = f32[5,4,8,1440]{3,2,1,0:T(8,128)S(1)} collective-permute-done((f32[5,4,8,1440]{3,2,1,0:T(8,128)S(1)}, f32[5,4,8,1440]{3,2,1,0:T(8,128)S(1)}, u32[]{:S(2)}, u32[]{:S(2)}) %collective-permute-start.9) | collective-permute-done | bytes 921632 | tf_op jit(solution)/shard_map/ppermute | solution.py:11
  186.7 42.6 %collective-permute-done.10 = f32[5,4,8,1440]{3,2,1,0:T(8,128)S(1)} collective-permute-done((f32[5,4,8,1440]{3,2,1,0:T(8,128)S(1)}, f32[5,4,8,1440]{3,2,1,0:T(8,128)S(1)}, u32[]{:S(2)}, u32[]{:S(2)}) %collective-permute-start.10) | collective-permute-done | bytes 921632 | tf_op jit(solution)/shard_map/ppermute | solution.py:11
  229.6 15.2 %collective-permute-done.11 = f32[5,4,8,1440]{3,2,1,0:T(8,128)S(1)} collective-permute-done((f32[5,4,8,1440]{3,2,1,0:T(8,128)S(1)}, f32[5,4,8,1440]{3,2,1,0:T(8,128)S(1)}, u32[]{:S(2)}, u32[]{:S(2)}) %collective-permute-start.11) | collective-permute-done | bytes 921632 | tf_op jit(solution)/shard_map/ppermute | solution.py:11
  252.6 3.5 %collective-permute-start.13 = (f32[6,4,8,3]{3,2,1,0:T(8,128)S(1)}, f32[6,4,8,3]{3,2,1,0:T(8,128)S(1)}, u32[]{:S(2)}, u32[]{:S(2)}) collective-permute-start(f32[6,4,8,3]{3,2,1,0:T(8,128)S(1)} %get-tuple-element.11), channel_id=1, source_target_pairs={{1,0},{2,1},{3,2},{4,3},{5,4},{6,5},{7,6},{0,7},{9,8},{10,9},{11,1... | collective-permute-start | bytes 6920 | tf_op jit(solution)/shard_map/ppermute | solution.py:24
  257.2 2.0 collective-permute-done.12
  259.2 1.7 concatenate.174
  263.4 3.4 %collective-permute-start.14 = (f32[6,4,3,1440]{3,1,2,0:T(4,128)S(1)}, f32[6,4,3,1440]{3,1,2,0:T(4,128)S(1)}, u32[]{:S(2)}, u32[]{:S(2)}) collective-permute-start(f32[6,4,3,1440]{3,1,2,0:T(4,128)S(1)} %copy.31), channel_id=1, source_target_pairs={{0,8},{8,16},{16,24},{1,9},{9,17},{17,25},{2,10},{10,18},{18,26},{... | collective-permute-start | bytes 1244168 | tf_op jit(solution)/shard_map/ppermute | solution.py:21
  267.0 1.3 collective-permute-start.15
  268.3 4.5 %collective-permute-done.14 = f32[6,4,3,1440]{3,1,2,0:T(4,128)S(1)} collective-permute-done((f32[6,4,3,1440]{3,1,2,0:T(4,128)S(1)}, f32[6,4,3,1440]{3,1,2,0:T(4,128)S(1)}, u32[]{:S(2)}, u32[]{:S(2)}) %collective-permute-start.14) | collective-permute-done | bytes 414752 | tf_op jit(solution)/shard_map/ppermute | solution.py:21
  273.0 10.0 %collective-permute-done.15 = f32[6,4,3,1440]{3,1,2,0:T(4,128)S(1)} collective-permute-done((f32[6,4,3,1440]{3,1,2,0:T(4,128)S(1)}, f32[6,4,3,1440]{3,1,2,0:T(4,128)S(1)}, u32[]{:S(2)}, u32[]{:S(2)}) %collective-permute-start.15) | collective-permute-done | bytes 414752 | tf_op jit(solution)/shard_map/ppermute | solution.py:24
  285.4 1.8 fusion.14
  (130 shorter events, 35.1 us)
Async XLA Ops:
  0.6 17.7 %copy-start.1 = (f32[4,4,8,1440]{3,2,1,0:T(8,128)S(1)}, f32[4,4,8,1440]{3,2,1,0:T(8,128)}, u32[]{:S(2)}) copy-start(f32[4,4,8,1440]{3,2,1,0:T(8,128)} %param.6) | copy-start | bytes 2211844
  0.6 17.7 %copy-start.2 = (f32[4,8,1440]{2,1,0:T(8,128)S(1)}, f32[4,8,1440]{2,1,0:T(8,128)}, u32[]{:S(2)}) copy-start(f32[4,8,1440]{2,1,0:T(8,128)} %param.5) | copy-start | bytes 552964
  0.7 1.8 copy-start.4
  2.0 16.3 %collective-permute-start = (f32[5,4,8,1440]{3,2,1,0:T(8,128)S(1)}, f32[5,4,8,1440]{3,2,1,0:T(8,128)S(1)}, u32[]{:S(2)}, u32[]{:S(2)}) collective-permute-start(f32[5,4,8,1440]{3,2,1,0:T(8,128)S(1)} %pad_maximum_fusion.16), channel_id=1, source_target_pairs={{0,1},{1,2},{2,3},{3,4},{4,5},{5,6},{6,7},{7,0},{8,9},{9,10},{10,1... | collective-permute-start | bytes 2764808 | tf_op jit(solution)/shard_map/ppermute | solution.py:11
  18.5 23.4 %collective-permute-start.1 = (f32[5,4,8,1440]{3,2,1,0:T(8,128)S(1)}, f32[5,4,8,1440]{3,2,1,0:T(8,128)S(1)}, u32[]{:S(2)}, u32[]{:S(2)}) collective-permute-start(f32[5,4,8,1440]{3,2,1,0:T(8,128)S(1)} %broadcast_select_fusion.1), channel_id=1, source_target_pairs={{0,2},{1,3},{2,4},{3,5},{4,6},{5,7},{6,0},{7,1},{8,10},{9,11},{10,... | collective-permute-start | bytes 2764808 | tf_op jit(solution)/shard_map/ppermute | solution.py:11
  42.1 43.0 %copy-start.3 = (f32[4,8,1440]{2,1,0:T(8,128)S(1)}, f32[4,8,1440]{2,1,0:T(8,128)}, u32[]{:S(2)}) copy-start(f32[4,8,1440]{2,1,0:T(8,128)} %param.8) | copy-start | bytes 552964
  42.1 42.7 %collective-permute-start.2 = (f32[5,4,8,1440]{3,2,1,0:T(8,128)S(1)}, f32[5,4,8,1440]{3,2,1,0:T(8,128)S(1)}, u32[]{:S(2)}, u32[]{:S(2)}) collective-permute-start(f32[5,4,8,1440]{3,2,1,0:T(8,128)S(1)} %broadcast_select_fusion.3), channel_id=1, source_target_pairs={{0,4},{1,5},{2,6},{3,7},{4,0},{5,1},{6,2},{7,3},{8,12},{9,13},{10,... | collective-permute-start | bytes 2764808 | tf_op jit(solution)/shard_map/ppermute | solution.py:11
  85.0 15.4 %collective-permute-start.3 = (f32[5,4,8,1440]{3,2,1,0:T(8,128)S(1)}, f32[5,4,8,1440]{3,2,1,0:T(8,128)S(1)}, u32[]{:S(2)}, u32[]{:S(2)}) collective-permute-start(f32[5,4,8,1440]{3,2,1,0:T(8,128)S(1)} %broadcast_select_fusion.5), channel_id=1, source_target_pairs={{0,1},{1,2},{2,3},{3,4},{4,5},{5,6},{6,7},{7,0},{8,9},{9,10},{10,1... | collective-permute-start | bytes 2764808 | tf_op jit(solution)/shard_map/ppermute | solution.py:11
  107.4 0.9 copy-start
  108.4 5.9 %collective-permute-start.4 = (f32[6,4,8,3]{3,2,1,0:T(8,128)S(1)}, f32[6,4,8,3]{3,2,1,0:T(8,128)S(1)}, u32[]{:S(2)}, u32[]{:S(2)}) collective-permute-start(f32[6,4,8,3]{3,2,1,0:T(8,128)S(1)} %get-tuple-element.18), channel_id=1, source_target_pairs={{0,1},{1,2},{2,3},{3,4},{4,5},{5,6},{6,7},{7,0},{8,9},{9,10},{10,1... | collective-permute-start | bytes 6920 | tf_op jit(solution)/shard_map/ppermute | solution.py:21
  108.5 5.8 %collective-permute-start.5 = (f32[6,4,8,3]{3,2,1,0:T(8,128)S(1)}, f32[6,4,8,3]{3,2,1,0:T(8,128)S(1)}, u32[]{:S(2)}, u32[]{:S(2)}) collective-permute-start(f32[6,4,8,3]{3,2,1,0:T(8,128)S(1)} %get-tuple-element.17), channel_id=1, source_target_pairs={{1,0},{2,1},{3,2},{4,3},{5,4},{6,5},{7,6},{0,7},{9,8},{10,9},{11,1... | collective-permute-start | bytes 6920 | tf_op jit(solution)/shard_map/ppermute | solution.py:24
  118.6 11.5 %collective-permute-start.6 = (f32[6,4,3,1440]{3,0,2,1:T(8,128)S(1)}, f32[6,4,3,1440]{3,0,2,1:T(8,128)S(1)}, u32[]{:S(2)}, u32[]{:S(2)}) collective-permute-start(f32[6,4,3,1440]{3,0,2,1:T(8,128)S(1)} %copy.23), channel_id=1, source_target_pairs={{0,8},{8,16},{16,24},{1,9},{9,17},{17,25},{2,10},{10,18},{18,26},{... | collective-permute-start | bytes 1244168 | tf_op jit(solution)/shard_map/ppermute | solution.py:21
  121.8 22.9 %collective-permute-start.7 = (f32[6,4,3,1440]{3,0,2,1:T(8,128)S(1)}, f32[6,4,3,1440]{3,0,2,1:T(8,128)S(1)}, u32[]{:S(2)}, u32[]{:S(2)}) collective-permute-start(f32[6,4,3,1440]{3,0,2,1:T(8,128)S(1)} %copy.24), channel_id=1, source_target_pairs={{8,0},{16,8},{24,16},{9,1},{17,9},{25,17},{10,2},{18,10},{26,18},{... | collective-permute-start | bytes 1244168 | tf_op jit(solution)/shard_map/ppermute | solution.py:24
  149.1 15.4 %collective-permute-start.8 = (f32[5,4,8,1440]{3,2,1,0:T(8,128)S(1)}, f32[5,4,8,1440]{3,2,1,0:T(8,128)S(1)}, u32[]{:S(2)}, u32[]{:S(2)}) collective-permute-start(f32[5,4,8,1440]{3,2,1,0:T(8,128)S(1)} %slice_subtract_fusion.2), channel_id=1, source_target_pairs={{0,1},{1,2},{2,3},{3,4},{4,5},{5,6},{6,7},{7,0},{8,9},{9,10},{10,1... | collective-permute-start | bytes 2764808 | tf_op jit(solution)/shard_map/ppermute | solution.py:11
  164.7 21.7 %collective-permute-start.9 = (f32[5,4,8,1440]{3,2,1,0:T(8,128)S(1)}, f32[5,4,8,1440]{3,2,1,0:T(8,128)S(1)}, u32[]{:S(2)}, u32[]{:S(2)}) collective-permute-start(f32[5,4,8,1440]{3,2,1,0:T(8,128)S(1)} %broadcast_select_fusion), channel_id=1, source_target_pairs={{0,2},{1,3},{2,4},{3,5},{4,6},{5,7},{6,0},{7,1},{8,10},{9,11},{10,... | collective-permute-start | bytes 2764808 | tf_op jit(solution)/shard_map/ppermute | solution.py:11
  186.7 42.6 %collective-permute-start.10 = (f32[5,4,8,1440]{3,2,1,0:T(8,128)S(1)}, f32[5,4,8,1440]{3,2,1,0:T(8,128)S(1)}, u32[]{:S(2)}, u32[]{:S(2)}) collective-permute-start(f32[5,4,8,1440]{3,2,1,0:T(8,128)S(1)} %broadcast_select_fusion.2), channel_id=1, source_target_pairs={{0,4},{1,5},{2,6},{3,7},{4,0},{5,1},{6,2},{7,3},{8,12},{9,13},{10,... | collective-permute-start | bytes 2764808 | tf_op jit(solution)/shard_map/ppermute | solution.py:11
  229.5 15.4 %collective-permute-start.11 = (f32[5,4,8,1440]{3,2,1,0:T(8,128)S(1)}, f32[5,4,8,1440]{3,2,1,0:T(8,128)S(1)}, u32[]{:S(2)}, u32[]{:S(2)}) collective-permute-start(f32[5,4,8,1440]{3,2,1,0:T(8,128)S(1)} %broadcast_select_fusion.4), channel_id=1, source_target_pairs={{0,1},{1,2},{2,3},{3,4},{4,5},{5,6},{6,7},{7,0},{8,9},{9,10},{10,1... | collective-permute-start | bytes 2764808 | tf_op jit(solution)/shard_map/ppermute | solution.py:11
  252.5 6.7 %collective-permute-start.12 = (f32[6,4,8,3]{3,2,1,0:T(8,128)S(1)}, f32[6,4,8,3]{3,2,1,0:T(8,128)S(1)}, u32[]{:S(2)}, u32[]{:S(2)}) collective-permute-start(f32[6,4,8,3]{3,2,1,0:T(8,128)S(1)} %get-tuple-element.12), channel_id=1, source_target_pairs={{0,1},{1,2},{2,3},{3,4},{4,5},{5,6},{6,7},{7,0},{8,9},{9,10},{10,1... | collective-permute-start | bytes 6920 | tf_op jit(solution)/shard_map/ppermute | solution.py:21
  252.6 6.6 %collective-permute-start.13 = (f32[6,4,8,3]{3,2,1,0:T(8,128)S(1)}, f32[6,4,8,3]{3,2,1,0:T(8,128)S(1)}, u32[]{:S(2)}, u32[]{:S(2)}) collective-permute-start(f32[6,4,8,3]{3,2,1,0:T(8,128)S(1)} %get-tuple-element.11), channel_id=1, source_target_pairs={{1,0},{2,1},{3,2},{4,3},{5,4},{6,5},{7,6},{0,7},{9,8},{10,9},{11,1... | collective-permute-start | bytes 6920 | tf_op jit(solution)/shard_map/ppermute | solution.py:24
  263.4 9.4 %collective-permute-start.14 = (f32[6,4,3,1440]{3,1,2,0:T(4,128)S(1)}, f32[6,4,3,1440]{3,1,2,0:T(4,128)S(1)}, u32[]{:S(2)}, u32[]{:S(2)}) collective-permute-start(f32[6,4,3,1440]{3,1,2,0:T(4,128)S(1)} %copy.31), channel_id=1, source_target_pairs={{0,8},{8,16},{16,24},{1,9},{9,17},{17,25},{2,10},{10,18},{18,26},{... | collective-permute-start | bytes 1244168 | tf_op jit(solution)/shard_map/ppermute | solution.py:21
  267.0 16.0 %collective-permute-start.15 = (f32[6,4,3,1440]{3,1,2,0:T(4,128)S(1)}, f32[6,4,3,1440]{3,1,2,0:T(4,128)S(1)}, u32[]{:S(2)}, u32[]{:S(2)}) collective-permute-start(f32[6,4,3,1440]{3,1,2,0:T(4,128)S(1)} %copy.32), channel_id=1, source_target_pairs={{8,0},{16,8},{24,16},{9,1},{17,9},{25,17},{10,2},{18,10},{26,18},{... | collective-permute-start | bytes 1244168 | tf_op jit(solution)/shard_map/ppermute | solution.py:24
where the time goes:
time: 289 us
  waiting for transfers between devices  229 us (79%)
  other arithmetic  29.4 us (10%)
  starting transfers between devices  18.4 us (6%)
  local copies, waits for them, and re-layouts  10.6 us (4%)
    ppermute x8, waiting for transfers between devices, from_behind(): lax.ppermute(array, axis, [(i, (i + by) % count) for i in range(count)])  190 us
    ppermute x4, waiting for transfers between devices, padded_2(): lax.ppermute(lax.slice_in_dim(block, 0, width, axis=dim), axis, backward)  24.3 us
    ppermute x4, waiting for transfers between devices, padded_2(): lax.ppermute(lax.slice_in_dim(block, block.shape[dim] - width, None, axis...  14.5 us
    select_n x22, other arithmetic, roll_rows(): result = jnp.where(picked[None, ..., None], rolled, result)  11.1 us
    ppermute x4, starting transfers between devices, padded_2(): lax.ppermute(lax.slice_in_dim(block, 0, width, axis=dim), axis, backward)  9.83 us
    ppermute x4, starting transfers between devices, padded_2(): lax.ppermute(lax.slice_in_dim(block, block.shape[dim] - width, None, axis...  6.47 us
  transfers between devices with their start and end apart: 16, of which 14 were waited for; matrix products, arithmetic and copies ran while one was open for 1% of the time, Pallas kernels for 0%

commit v1 on v0

v1 whole, which is shorter than its diff:
```python
import functools

import jax
import jax.numpy as jnp
from jax import lax
from jax.experimental import pallas as pl
from jax.experimental.pallas import tpu as pltpu
from jax.sharding import PartitionSpec as P

ITERS = 2
HALO = 3
LANES = 128


def round_up(value, unit=LANES):
    return -(-value // unit) * unit


def exchange(array, stride):
    count = lax.axis_size("lon")
    return lax.ppermute(array, "lon", [(i, i ^ stride) for i in range(count)])


def lat_halos(block, dim):
    count = lax.axis_size("lat")
    forward = [(i, i + 1) for i in range(count - 1)]
    backward = [(b, a) for a, b in forward]
    size = block.shape[dim]
    south = lax.ppermute(lax.slice_in_dim(block, size - HALO, size, axis=dim), "lat", forward)
    north = lax.ppermute(lax.slice_in_dim(block, 0, HALO, axis=dim), "lat", backward)
    return south, north


def right_amount(centre, left_edge, right_edge, fraction):
    slope = right_edge - left_edge
    curve = 6.0 * centre - 3.0 * (left_edge + right_edge)
    return fraction * (
        right_edge - 0.5 * fraction * (slope - (1.0 - fraction * (2.0 / 3.0)) * curve)
    )


def left_amount(centre, left_edge, right_edge, fraction):
    slope = right_edge - left_edge
    curve = 6.0 * centre - 3.0 * (left_edge + right_edge)
    return fraction * (
        left_edge + 0.5 * fraction * (slope + (1.0 - fraction * (2.0 / 3.0)) * curve)
    )


def window_kernel(held, lead, width, plan, *refs):
    own = refs[:held]
    other = refs[held : 2 * held]
    mine, theirs, joined = refs[2 * held :]
    comps, band, _ = mine.shape
    out_width = mine.shape[2]

    def fill(low, high):
        for t in range(held):
            joined[t, :, :, lead : lead + width] = low[t][...]
            joined[t, :, :, lead + width : lead + 2 * width] = high[t][...]

    core = plan[0, 0]

    @pl.when(core == 0)
    def _():
        fill(own, other)

    @pl.when(core != 0)
    def _():
        fill(other, own)

    lane = lax.broadcasted_iota(jnp.int32, (comps, 1, LANES), 2)
    for target, out in ((1, mine), (3, theirs)):
        for j in range(band):
            slot = plan[target, j]
            first = plan[target + 1, j]
            begin = lead + jnp.maximum(first, -lead)
            tile = begin // LANES
            rest = begin - tile * LANES
            back = jnp.where(rest == 0, 0, LANES - rest)

            def piece(m):
                values = joined[slot, :, j : j + 1, pl.ds(pl.multiple_of((tile + m) * LANES, LANES), LANES)]
                return pltpu.roll(values, back, 2)

            now = piece(0)
            for m in range(out_width // LANES):
                later = piece(m + 1)
                values = jnp.where(lane < LANES - rest, now, later)
                place = lane + (first + m * LANES)
                inside = (place >= 0) & (place < 2 * width)
                out[:, j : j + 1, m * LANES : (m + 1) * LANES] = jnp.where(inside, values, 0.0)
                now = later


def cut_windows(own, other, plan):
    held = len(own)
    comps, band, width = own[0].shape
    out_width = round_up(width + 2 * HALO)
    lead = out_width
    total = round_up(lead + 2 * width) + out_width + 2 * LANES
    shape = jax.ShapeDtypeStruct((comps, band, out_width), jnp.float32)
    return pl.pallas_call(
        functools.partial(window_kernel, held, lead, width),
        out_shape=(shape, shape),
        in_specs=[pl.BlockSpec(memory_space=pltpu.SMEM)]
        + [pl.BlockSpec(memory_space=pltpu.VMEM)] * (2 * held),
        out_specs=(pl.BlockSpec(memory_space=pltpu.VMEM),) * 2,
        scratch_shapes=[pltpu.VMEM((held, comps, band, total), jnp.float32)],
        compiler_params=pltpu.CompilerParams(vmem_limit_bytes=32 * 1024 * 1024),
        cost_estimate=pl.CostEstimate(flops=2_000_000, bytes_accessed=2_000_000, transcendentals=0),
        name="cut_windows",
    )(plan, *own, *other)


def zonal_kernel(mine, theirs, frac, out):
    comps, band, width = out.shape
    full = mine.shape[2]
    fraction = frac[...]
    for c in range(comps):
        w = mine[c] + theirs[c]
        w_1 = pltpu.roll(w, 1, 1)
        w_2 = pltpu.roll(w, 2, 1)
        w1 = pltpu.roll(w, full - 1, 1)
        face = (7.0 * (w_1 + w) - (w_2 + w1)) / 12.0
        flux = right_amount(w_1, pltpu.roll(face, 1, 1), face, fraction)
        new = w + flux - pltpu.roll(flux, full - 1, 1)
        out[c] = pltpu.roll(new, full - HALO, 1)[:, :width]


def zonal(mine, theirs, frac, width):
    comps, band, _ = mine.shape
    return pl.pallas_call(
        zonal_kernel,
        out_shape=jax.ShapeDtypeStruct((comps, band, width), jnp.float32),
        cost_estimate=pl.CostEstimate(flops=2_000_000, bytes_accessed=1_000_000, transcendentals=0),
        name="zonal",
    )(mine, theirs, frac)


def merid_kernel(fields, south, north, courant, out):
    comps, band, width = out.shape
    step = 2 * LANES
    for at in range(0, width, step):
        cols = slice(at, min(at + step, width))
        g = courant[HALO : HALO + band + 1, cols]
        northward = jnp.maximum(g, 0.0)
        southward = jnp.maximum(-g, 0.0)
        for c in range(comps):
            padded = jnp.concatenate([south[c, :, cols], fields[c, :, cols], north[c, :, cols]], axis=0)
            faces = (7.0 * (padded[1:-2] + padded[2:-1]) - (padded[:-3] + padded[3:])) / 12.0
            flux = right_amount(
                padded[2 : band + 3], faces[0 : band + 1], faces[1 : band + 2], northward
            ) - left_amount(
                padded[3 : band + 4], faces[1 : band + 2], faces[2 : band + 3], southward
            )
            out[c, :, cols] = padded[3 : band + 3] + flux[:band] - flux[1:]


def merid(fields, south, north, courant):
    return pl.pallas_call(
        merid_kernel,
        out_shape=jax.ShapeDtypeStruct(fields.shape, jnp.float32),
        cost_estimate=pl.CostEstimate(flops=4_000_000, bytes_accessed=1_000_000, transcendentals=0),
        name="merid",
    )(fields, south, north, courant)


def make_plan(shift, width, count, me):
    full = width * count
    parity = me // 2 % 2

    def towards(device):
        begin = jnp.mod(device * width - HALO - shift, full)
        pair = begin // (2 * width)
        offset = begin - pair * (2 * width)
        here = pair % 2 == parity
        chosen = jnp.where(here, pair, (pair + 1) % (count // 2))
        slot = (chosen // 2) ^ (me // 4)
        return [slot, jnp.where(here, offset, offset - 2 * width)]

    core = jnp.broadcast_to(me % 2, shift.shape)
    rows = [core] + towards(me) + towards(me ^ 2)
    return jnp.stack(rows, axis=1).astype(jnp.int32)


def local(air_mass, tracer_mass, zonal_frac, merid_courant, zonal_shift):
    levels, band, width = air_mass.shape
    count = lax.axis_size("lon")
    me = lax.axis_index("lon")
    global_row = lax.axis_index("lat") * band + jnp.arange(band, dtype=jnp.int32)
    courant = jnp.where(
        global_row[None, :, None] == 0, jnp.zeros_like(merid_courant), merid_courant
    )
    plan = make_plan(zonal_shift, width, count, me)

    ring = [(i, (i + 1) % count) for i in range(count)]
    west = lax.ppermute(zonal_frac[..., width - HALO :], "lon", ring)
    east = lax.ppermute(zonal_frac[..., :HALO], "lon", [(b, a) for a, b in ring])
    out_width = round_up(width + 2 * HALO)
    fill = jnp.zeros((levels, band, out_width - width - 2 * HALO), jnp.float32)
    frac = jnp.concatenate([west, zonal_frac, east, fill], axis=2)
    south, north = lat_halos(courant, 1)
    courant = jnp.concatenate([south, courant, north], axis=1)

    fields = [
        jnp.concatenate([air_mass[None, l], tracer_mass[:, l]], axis=0) for l in range(levels)
    ]
    for step in range(ITERS):
        held = [[f] for f in fields]
        stride = 4
        while stride < count:
            for l in range(levels):
                held[l] = held[l] + [exchange(x, stride) for x in held[l]]
            stride *= 2
        for l in range(levels):
            other = [exchange(x, 1) for x in held[l]]
            mine, theirs = cut_windows(held[l], other, plan[l])
            theirs = exchange(theirs, 2)
            moved = zonal(mine, theirs, frac[l], width)
            south, north = lat_halos(moved, 1)
            fields[l] = merid(moved, south, north, courant[l])
    result = jnp.stack(fields, axis=1)
    return (result[0], result[1:])


def solution(mesh):
    return jax.shard_map(
        local,
        mesh=mesh,
        in_specs=(
            P(None, "lat", "lon"),
            P(None, None, "lat", "lon"),
            P(None, "lat", "lon"),
            P(None, "lat", "lon"),
            P(None, "lat"),
        ),
        out_specs=(P(None, "lat", "lon"), P(None, None, "lat", "lon")),
        check_vma=False,
    )
```

time: 289 us -> 221 us (0.76); the launches traced: 289 us -> 218 us
  waiting for transfers between devices: 229 us -> 39 us
  starting transfers between devices: 18.4 us -> 91.6 us
  Pallas kernels: 0 us -> 58.3 us
  other arithmetic: 29.4 us -> 2.16 us
  local copies, waits for them, and re-layouts: 10.6 us -> 25.1 us
    ppermute x16 -> x52, waiting for transfers between devices: 229 us -> 39 us  [the longest x32 38.9 us: exchange(): return lax.ppermute(array, 'lon', [(i, i ^ stride) for i in range(count)])]
    ppermute x16 -> x52, starting transfers between devices: 18.4 us -> 91.6 us  [the longest x9 45 us: lat_halos(): lax.ppermute(lax.slice_in_dim(block, size - HALO, size, axis=dim), 'lat',...]
    pallas_call x0 -> x24, Pallas kernels: none -> 58.3 us  [the longest x8 21.3 us: zonal(): pl.pallas_call(zonal_kernel, out_shape=jax.ShapeDtypeStruct((comps, band,...]
    unnamed x10 -> x96, local copies, waits for them, and re-layouts: 0.35 us -> 14.3 us
    select_n x28 -> x1, other arithmetic: 12.3 us -> 0.08 us  [local(): jnp.where(global_row[None, :, None] == 0, jnp.zeros_like(merid_courant),...]
    concatenate x15 -> x5, other arithmetic: 7.57 us -> 0.15 us  [the longest x4 0.08 us: local(): jnp.concatenate([air_mass[None, l], tracer_mass[:, l]], axis=0)]
    sub x6 -> x0, other arithmetic: 4.72 us -> none  [the longest x2 3.55 us: merid_update(): fluxes - left_amount(padded[..., 3:cells + 4, :], faces[..., 1:cells + 2,...]
    concatenate x2 -> x1, local copies, waits for them, and re-layouts: 3.43 us -> 0.15 us  [local(): frac = jnp.concatenate([west, zonal_frac, east, fill], axis=2)]
  transfers between devices with their start and end apart: 16 -> 52, of which waited for: 14 -> 6; matrix products, arithmetic and copies ran while one was open for 1% -> 5% of each run, Pallas kernels for 0% -> 26%
where the time goes in v1:
time: 221 us; the launch traced here: 218 us
  starting transfers between devices  91.6 us (41%)
  Pallas kernels  58.3 us (26%)
  waiting for transfers between devices  39 us (18%)
  local copies, waits for them, and re-layouts  25.1 us (11%)
    ppermute x9, starting transfers between devices, lat_halos(): lax.ppermute(lax.slice_in_dim(block, size - HALO, size, axis=dim), 'lat',...  45 us
    ppermute x32, waiting for transfers between devices, exchange(): return lax.ppermute(array, 'lon', [(i, i ^ stride) for i in range(count)])  38.9 us
    ppermute x32, starting transfers between devices, exchange(): return lax.ppermute(array, 'lon', [(i, i ^ stride) for i in range(count)])  31 us
    pallas_call x8, Pallas kernels, zonal(): pl.pallas_call(zonal_kernel, out_shape=jax.ShapeDtypeStruct((comps, band,...  21.3 us
    pallas_call x8, Pallas kernels, merid(): pl.pallas_call(merid_kernel, out_shape=jax.ShapeDtypeStruct(fields.shape,...  21.2 us
    pallas_call x8, Pallas kernels, cut_windows(): pl.pallas_call(functools.partial(window_kernel, held, lead, width), out_s...  15.8 us
    unnamed x96, local copies, waits for them, and re-layouts  14.3 us
    ppermute x9, starting transfers between devices, lat_halos(): lax.ppermute(lax.slice_in_dim(block, 0, HALO, axis=dim), 'lat', backward)  12 us
  transfers between devices with their start and end apart: 52, of which 6 were waited for; matrix products, arithmetic and copies ran while one was open for 5% of the time, Pallas kernels for 26%

profile of v1, /device:TPU:0, one launch (start us, length us, event | category | flops | bytes accessed | tf_op | source)
XLA Modules:
  0.0 217.7 jit_solution(329827531171711134)
XLA Ops:
  2.0 4.1 %collective-permute-start = (f32[5,8,1440]{2,1,0:T(8,128)S(1)}, f32[5,8,1440]{2,1,0:T(8,128)S(1)}, u32[]{:S(2)}, u32[]{:S(2)}) collective-permute-start(f32[5,8,1440]{2,1,0:T(8,128)S(1)} %pad_maximum_fusion.4.refs_0_), channel_id=1, source_target_pairs={{0,4},{1,5},{2,6},{3,7},{4,0},{5,1},{6,2},{7,3},{8,12},{9,13},{10,... | collective-permute-start | bytes 691208 | tf_op jit(solution)/shard_map/ppermute | solution.py:21
  6.7 3.0 %collective-permute-start.5 = (f32[4,8,3]{2,1,0:T(8,128)S(1)}, f32[4,8,3]{2,1,0:T(8,128)S(1)}, u32[]{:S(2)}, u32[]{:S(2)}) collective-permute-start(f32[4,8,3]{2,1,0:T(8,128)S(1)} %get-tuple-element.70), channel_id=1, source_target_pairs={{1,0},{2,1},{3,2},{4,3},{5,4},{6,5},{7,6},{0,7},{9,8},{10,9},{11,1... | collective-permute-start | bytes 1160 | tf_op jit(solution)/shard_map/ppermute | solution.py:199
  9.9 3.4 %collective-permute-start.8 = (f32[4,3,1440]{2,1,0:T(4,128)S(1)}, f32[4,3,1440]{2,1,0:T(4,128)S(1)}, u32[]{:S(2)}, u32[]{:S(2)}) collective-permute-start(f32[4,3,1440]{2,1,0:T(4,128)S(1)} %get-tuple-element.68), channel_id=1, source_target_pairs={{0,8},{8,16},{16,24},{1,9},{9,17},{17,25},{2,10},{10,18},{18,26},{... | collective-permute-start | bytes 207368 | tf_op jit(solution)/shard_map/ppermute | solution.py:29
  15.7 8.7 %collective-permute-start.16 = (f32[5,8,1440]{2,1,0:T(8,128)S(1)}, f32[5,8,1440]{2,1,0:T(8,128)S(1)}, u32[]{:S(2)}, u32[]{:S(2)}) collective-permute-start(f32[5,8,1440]{2,1,0:T(8,128)S(1)} %pad_maximum_fusion.5.refs_0_), channel_id=1, source_target_pairs={{0,4},{1,5},{2,6},{3,7},{4,0},{5,1},{6,2},{7,3},{8,12},{9,13},{10,... | collective-permute-start | bytes 691208 | tf_op jit(solution)/shard_map/ppermute | solution.py:21
  25.3 4.3 %collective-permute-start.28 = (f32[5,8,1440]{2,1,0:T(8,128)S(1)}, f32[5,8,1440]{2,1,0:T(8,128)S(1)}, u32[]{:S(2)}, u32[]{:S(2)}) collective-permute-start(f32[5,8,1440]{2,1,0:T(8,128)S(1)} %pad_maximum_fusion.6.refs_0_), channel_id=1, source_target_pairs={{0,4},{1,5},{2,6},{3,7},{4,0},{5,1},{6,2},{7,3},{8,12},{9,13},{10,... | collective-permute-start | bytes 691208 | tf_op jit(solution)/shard_map/ppermute | solution.py:21
  29.6 14.2 %collective-permute-done.16.refs_1_ = f32[5,8,1440]{2,1,0:T(8,128)S(1)} collective-permute-done((f32[5,8,1440]{2,1,0:T(8,128)S(1)}, f32[5,8,1440]{2,1,0:T(8,128)S(1)}, u32[]{:S(2)}, u32[]{:S(2)}) %collective-permute-start.16) | collective-permute-done | bytes 230432 | tf_op jit(solution)/shard_map/ppermute | solution.py:21
  49.2 2.7 %collective-permute-done.40.refs_1_ = f32[5,8,1440]{2,1,0:T(8,128)S(1)} collective-permute-done((f32[5,8,1440]{2,1,0:T(8,128)S(1)}, f32[5,8,1440]{2,1,0:T(8,128)S(1)}, u32[]{:S(2)}, u32[]{:S(2)}) %collective-permute-start.40) | collective-permute-done | bytes 230432 | tf_op jit(solution)/shard_map/ppermute | solution.py:21
  65.5 2.7 %zonal.8.fields = f32[5,8,1440]{2,1,0:T(8,128)} custom-call(f32[5,8,1536]{2,1,0:T(8,128)} %copy-done.5, f32[5,8,1536]{2,1,0:T(8,128)} %copy-done.24, f32[8,1536]{1,0:T(8,128)} %get-tuple-element.60.frac), custom_call_target="tpu_custom_call" | custom-call | flops 2000000 | bytes 1000000 | tf_op jit(solution)/shard_map/zonal/pallas_call | solution.py:133
  69.2 4.3 %collective-permute-start.6 = (f32[5,3,1440]{2,1,0:T(4,128)S(1)}, f32[5,3,1440]{2,1,0:T(4,128)S(1)}, u32[]{:S(2)}, u32[]{:S(2)}) collective-permute-start(f32[5,3,1440]{2,1,0:T(4,128)S(1)} %get-tuple-element.47), channel_id=1, source_target_pairs={{0,8},{8,16},{16,24},{1,9},{9,17},{17,25},{2,10},{10,18},{18,26},{... | collective-permute-start | bytes 259208 | tf_op jit(solution)/shard_map/ppermute | solution.py:29
  79.3 4.9 %collective-permute-start.20 = (f32[5,3,1440]{2,1,0:T(4,128)S(1)}, f32[5,3,1440]{2,1,0:T(4,128)S(1)}, u32[]{:S(2)}, u32[]{:S(2)}) collective-permute-start(f32[5,3,1440]{2,1,0:T(4,128)S(1)} %get-tuple-element.51), channel_id=1, source_target_pairs={{0,8},{8,16},{16,24},{1,9},{9,17},{17,25},{2,10},{10,18},{18,26},{... | collective-permute-start | bytes 259208 | tf_op jit(solution)/shard_map/ppermute | solution.py:29
  89.4 5.4 %collective-permute-start.32 = (f32[5,3,1440]{2,1,0:T(4,128)S(1)}, f32[5,3,1440]{2,1,0:T(4,128)S(1)}, u32[]{:S(2)}, u32[]{:S(2)}) collective-permute-start(f32[5,3,1440]{2,1,0:T(4,128)S(1)} %get-tuple-element.55), channel_id=1, source_target_pairs={{0,8},{8,16},{16,24},{1,9},{9,17},{17,25},{2,10},{10,18},{18,26},{... | collective-permute-start | bytes 259208 | tf_op jit(solution)/shard_map/ppermute | solution.py:29
  94.8 2.7 %zonal.14.fields = f32[5,8,1440]{2,1,0:T(8,128)} custom-call(f32[5,8,1536]{2,1,0:T(8,128)} %copy-done.10, f32[5,8,1536]{2,1,0:T(8,128)} %copy-done.22, f32[8,1536]{1,0:T(8,128)} %get-tuple-element.61.frac), custom_call_target="tpu_custom_call" | custom-call | flops 2000000 | bytes 1000000 | tf_op jit(solution)/shard_map/zonal/pallas_call | solution.py:133
  103.0 2.7 %merid.10.refs_0_ = f32[5,8,1440]{2,1,0:T(8,128)} custom-call(f32[5,8,1440]{2,1,0:T(8,128)} %zonal.10.fields, f32[5,3,1440]{2,1,0:T(4,128)} %copy-done.33, f32[5,3,1440]{2,1,0:T(4,128)} %copy-done.38, f32[14,1440]{1,0:T(8,128)} %get-tuple-element.43.courant), custom_call_target="tpu_custom_call" | custom-call | flops 4000000 | bytes 1000000 | tf_op jit(solution)/shard_map/merid/pallas_call | solution.py:161
  105.7 2.9 %collective-permute-start.22 = (f32[5,8,1440]{2,1,0:T(8,128)}, f32[5,8,1440]{2,1,0:T(8,128)S(1)}, u32[]{:S(2)}, u32[]{:S(2)}) collective-permute-start(f32[5,8,1440]{2,1,0:T(8,128)} %merid.10.refs_0_), channel_id=1, source_target_pairs={{0,4},{1,5},{2,6},{3,7},{4,0},{5,1},{6,2},{7,3},{8,12},{9,13},{10,... | collective-permute-start | bytes 691208 | tf_op jit(solution)/shard_map/ppermute | solution.py:21
  108.6 5.4 %collective-permute-start.44 = (f32[5,3,1440]{2,1,0:T(4,128)S(1)}, f32[5,3,1440]{2,1,0:T(4,128)S(1)}, u32[]{:S(2)}, u32[]{:S(2)}) collective-permute-start(f32[5,3,1440]{2,1,0:T(4,128)S(1)} %get-tuple-element.59), channel_id=1, source_target_pairs={{0,8},{8,16},{16,24},{1,9},{9,17},{17,25},{2,10},{10,18},{18,26},{... | collective-permute-start | bytes 259208 | tf_op jit(solution)/shard_map/ppermute | solution.py:29
  115.4 4.4 %collective-permute-done.10.refs_1_ = f32[5,8,1440]{2,1,0:T(8,128)S(1)} collective-permute-done((f32[5,8,1440]{2,1,0:T(8,128)}, f32[5,8,1440]{2,1,0:T(8,128)S(1)}, u32[]{:S(2)}, u32[]{:S(2)}) %collective-permute-start.10) | collective-permute-done | bytes 230432 | tf_op jit(solution)/shard_map/ppermute | solution.py:21
  119.9 2.7 %merid.12.refs_0_ = f32[5,8,1440]{2,1,0:T(8,128)} custom-call(f32[5,8,1440]{2,1,0:T(8,128)} %zonal.12.fields, f32[5,3,1440]{2,1,0:T(4,128)} %copy-done.30, f32[5,3,1440]{2,1,0:T(4,128)} %copy-done.35, f32[14,1440]{1,0:T(8,128)} %get-tuple-element.42.courant), custom_call_target="tpu_custom_call" | custom-call | flops 4000000 | bytes 1000000 | tf_op jit(solution)/shard_map/merid/pallas_call | solution.py:161
  123.8 2.7 %merid.14.refs_0_ = f32[5,8,1440]{2,1,0:T(8,128)} custom-call(f32[5,8,1440]{2,1,0:T(8,128)} %zonal.14.fields, f32[5,3,1440]{2,1,0:T(4,128)} %copy-done.41, f32[5,3,1440]{2,1,0:T(4,128)} %copy-done.43, f32[14,1440]{1,0:T(8,128)} %get-tuple-element.41.courant), custom_call_target="tpu_custom_call" | custom-call | flops 4000000 | bytes 1000000 | tf_op jit(solution)/shard_map/merid/pallas_call | solution.py:161
  132.1 9.7 %collective-permute-done.34.refs_1_ = f32[5,8,1440]{2,1,0:T(8,128)S(1)} collective-permute-done((f32[5,8,1440]{2,1,0:T(8,128)}, f32[5,8,1440]{2,1,0:T(8,128)S(1)}, u32[]{:S(2)}, u32[]{:S(2)}) %collective-permute-start.34) | collective-permute-done | bytes 230432 | tf_op jit(solution)/shard_map/ppermute | solution.py:21
  141.8 5.2 %collective-permute-done.46.refs_1_ = f32[5,8,1440]{2,1,0:T(8,128)S(1)} collective-permute-done((f32[5,8,1440]{2,1,0:T(8,128)}, f32[5,8,1440]{2,1,0:T(8,128)S(1)}, u32[]{:S(2)}, u32[]{:S(2)}) %collective-permute-start.46) | collective-permute-done | bytes 230432 | tf_op jit(solution)/shard_map/ppermute | solution.py:21
  162.1 5.2 %collective-permute-start.14 = (f32[5,3,1440]{2,1,0:T(4,128)S(1)}, f32[5,3,1440]{2,1,0:T(4,128)S(1)}, u32[]{:S(2)}, u32[]{:S(2)}) collective-permute-start(f32[5,3,1440]{2,1,0:T(4,128)S(1)} %get-tuple-element.45), channel_id=1, source_target_pairs={{0,8},{8,16},{16,24},{1,9},{9,17},{17,25},{2,10},{10,18},{18,26},{... | collective-permute-start | bytes 259208 | tf_op jit(solution)/shard_map/ppermute | solution.py:29
  173.2 5.4 %collective-permute-start.26 = (f32[5,3,1440]{2,1,0:T(4,128)S(1)}, f32[5,3,1440]{2,1,0:T(4,128)S(1)}, u32[]{:S(2)}, u32[]{:S(2)}) collective-permute-start(f32[5,3,1440]{2,1,0:T(4,128)S(1)} %get-tuple-element.49), channel_id=1, source_target_pairs={{0,8},{8,16},{16,24},{1,9},{9,17},{17,25},{2,10},{10,18},{18,26},{... | collective-permute-start | bytes 259208 | tf_op jit(solution)/shard_map/ppermute | solution.py:29
  183.8 5.4 %collective-permute-start.38 = (f32[5,3,1440]{2,1,0:T(4,128)S(1)}, f32[5,3,1440]{2,1,0:T(4,128)S(1)}, u32[]{:S(2)}, u32[]{:S(2)}) collective-permute-start(f32[5,3,1440]{2,1,0:T(4,128)S(1)} %get-tuple-element.53), channel_id=1, source_target_pairs={{0,8},{8,16},{16,24},{1,9},{9,17},{17,25},{2,10},{10,18},{18,26},{... | collective-permute-start | bytes 259208 | tf_op jit(solution)/shard_map/ppermute | solution.py:29
  194.4 5.4 %collective-permute-start.50 = (f32[5,3,1440]{2,1,0:T(4,128)S(1)}, f32[5,3,1440]{2,1,0:T(4,128)S(1)}, u32[]{:S(2)}, u32[]{:S(2)}) collective-permute-start(f32[5,3,1440]{2,1,0:T(4,128)S(1)} %get-tuple-element.57), channel_id=1, source_target_pairs={{0,8},{8,16},{16,24},{1,9},{9,17},{17,25},{2,10},{10,18},{18,26},{... | collective-permute-start | bytes 259208 | tf_op jit(solution)/shard_map/ppermute | solution.py:29
  (230 shorter events, 98.4 us)
Async XLA Ops:
  2.0 27.5 %collective-permute-start = (f32[5,8,1440]{2,1,0:T(8,128)S(1)}, f32[5,8,1440]{2,1,0:T(8,128)S(1)}, u32[]{:S(2)}, u32[]{:S(2)}) collective-permute-start(f32[5,8,1440]{2,1,0:T(8,128)S(1)} %pad_maximum_fusion.4.refs_0_), channel_id=1, source_target_pairs={{0,4},{1,5},{2,6},{3,7},{4,0},{5,1},{6,2},{7,3},{8,12},{9,13},{10,... | collective-permute-start | bytes 691208 | tf_op jit(solution)/shard_map/ppermute | solution.py:21
  6.1 23.5 %collective-permute-start.1 = (f32[5,8,1440]{2,1,0:T(8,128)S(1)}, f32[5,8,1440]{2,1,0:T(8,128)S(1)}, u32[]{:S(2)}, u32[]{:S(2)}) collective-permute-start(f32[5,8,1440]{2,1,0:T(8,128)S(1)} %pad_maximum_fusion.4.refs_0_), channel_id=1, source_target_pairs={{0,1},{1,0},{2,3},{3,2},{4,5},{5,4},{6,7},{7,6},{8,9},{9,8},{10,11... | collective-permute-start | bytes 691208 | tf_op jit(solution)/shard_map/ppermute | solution.py:21
  15.7 28.2 %collective-permute-start.16 = (f32[5,8,1440]{2,1,0:T(8,128)S(1)}, f32[5,8,1440]{2,1,0:T(8,128)S(1)}, u32[]{:S(2)}, u32[]{:S(2)}) collective-permute-start(f32[5,8,1440]{2,1,0:T(8,128)S(1)} %pad_maximum_fusion.5.refs_0_), channel_id=1, source_target_pairs={{0,4},{1,5},{2,6},{3,7},{4,0},{5,1},{6,2},{7,3},{8,12},{9,13},{10,... | collective-permute-start | bytes 691208 | tf_op jit(solution)/shard_map/ppermute | solution.py:21
  25.3 21.3 %collective-permute-start.17 = (f32[5,8,1440]{2,1,0:T(8,128)S(1)}, f32[5,8,1440]{2,1,0:T(8,128)S(1)}, u32[]{:S(2)}, u32[]{:S(2)}) collective-permute-start(f32[5,8,1440]{2,1,0:T(8,128)S(1)} %pad_maximum_fusion.5.refs_0_), channel_id=1, source_target_pairs={{0,1},{1,0},{2,3},{3,2},{4,5},{5,4},{6,7},{7,6},{8,9},{9,8},{10,11... | collective-permute-start | bytes 691208 | tf_op jit(solution)/shard_map/ppermute | solution.py:21
  25.3 23.9 %collective-permute-start.28 = (f32[5,8,1440]{2,1,0:T(8,128)S(1)}, f32[5,8,1440]{2,1,0:T(8,128)S(1)}, u32[]{:S(2)}, u32[]{:S(2)}) collective-permute-start(f32[5,8,1440]{2,1,0:T(8,128)S(1)} %pad_maximum_fusion.6.refs_0_), channel_id=1, source_target_pairs={{0,4},{1,5},{2,6},{3,7},{4,0},{5,1},{6,2},{7,3},{8,12},{9,13},{10,... | collective-permute-start | bytes 691208 | tf_op jit(solution)/shard_map/ppermute | solution.py:21
  29.6 22.3 %collective-permute-start.40 = (f32[5,8,1440]{2,1,0:T(8,128)S(1)}, f32[5,8,1440]{2,1,0:T(8,128)S(1)}, u32[]{:S(2)}, u32[]{:S(2)}) collective-permute-start(f32[5,8,1440]{2,1,0:T(8,128)S(1)} %pad_maximum_fusion.7.refs_0_), channel_id=1, source_target_pairs={{0,4},{1,5},{2,6},{3,7},{4,0},{5,1},{6,2},{7,3},{8,12},{9,13},{10,... | collective-permute-start | bytes 691208 | tf_op jit(solution)/shard_map/ppermute | solution.py:21
  55.3 19.5 %collective-permute-start.19 = (f32[5,8,1536]{2,1,0:T(8,128)S(1)}, f32[5,8,1536]{2,1,0:T(8,128)S(1)}, u32[]{:S(2)}, u32[]{:S(2)}) collective-permute-start(f32[5,8,1536]{2,1,0:T(8,128)S(1)} %get-tuple-element.23), channel_id=1, source_target_pairs={{0,2},{1,3},{2,0},{3,1},{4,6},{5,7},{6,4},{7,5},{8,10},{9,11},{10,... | collective-permute-start | bytes 737288 | tf_op jit(solution)/shard_map/ppermute | solution.py:21
  60.0 24.2 %collective-permute-start.31 = (f32[5,8,1536]{2,1,0:T(8,128)S(1)}, f32[5,8,1536]{2,1,0:T(8,128)S(1)}, u32[]{:S(2)}, u32[]{:S(2)}) collective-permute-start(f32[5,8,1536]{2,1,0:T(8,128)S(1)} %get-tuple-element.27), channel_id=1, source_target_pairs={{0,2},{1,3},{2,0},{3,1},{4,6},{5,7},{6,4},{7,5},{8,10},{9,11},{10,... | collective-permute-start | bytes 737288 | tf_op jit(solution)/shard_map/ppermute | solution.py:21
  62.7 26.6 %collective-permute-start.43 = (f32[5,8,1536]{2,1,0:T(8,128)S(1)}, f32[5,8,1536]{2,1,0:T(8,128)S(1)}, u32[]{:S(2)}, u32[]{:S(2)}) collective-permute-start(f32[5,8,1536]{2,1,0:T(8,128)S(1)} %get-tuple-element.31), channel_id=1, source_target_pairs={{0,2},{1,3},{2,0},{3,1},{4,6},{5,7},{6,4},{7,5},{8,10},{9,11},{10,... | collective-permute-start | bytes 737288 | tf_op jit(solution)/shard_map/ppermute | solution.py:21
  69.2 28.3 %collective-permute-start.6 = (f32[5,3,1440]{2,1,0:T(4,128)S(1)}, f32[5,3,1440]{2,1,0:T(4,128)S(1)}, u32[]{:S(2)}, u32[]{:S(2)}) collective-permute-start(f32[5,3,1440]{2,1,0:T(4,128)S(1)} %get-tuple-element.47), channel_id=1, source_target_pairs={{0,8},{8,16},{16,24},{1,9},{9,17},{17,25},{2,10},{10,18},{18,26},{... | collective-permute-start | bytes 259208 | tf_op jit(solution)/shard_map/ppermute | solution.py:29
  73.5 25.5 %collective-permute-start.7 = (f32[5,3,1440]{2,1,0:T(4,128)S(1)}, f32[5,3,1440]{2,1,0:T(4,128)S(1)}, u32[]{:S(2)}, u32[]{:S(2)}) collective-permute-start(f32[5,3,1440]{2,1,0:T(4,128)S(1)} %get-tuple-element.46), channel_id=1, source_target_pairs={{8,0},{16,8},{24,16},{9,1},{17,9},{25,17},{10,2},{18,10},{26,18},{... | collective-permute-start | bytes 259208 | tf_op jit(solution)/shard_map/ppermute | solution.py:30
  79.3 23.0 %collective-permute-start.20 = (f32[5,3,1440]{2,1,0:T(4,128)S(1)}, f32[5,3,1440]{2,1,0:T(4,128)S(1)}, u32[]{:S(2)}, u32[]{:S(2)}) collective-permute-start(f32[5,3,1440]{2,1,0:T(4,128)S(1)} %get-tuple-element.51), channel_id=1, source_target_pairs={{0,8},{8,16},{16,24},{1,9},{9,17},{17,25},{2,10},{10,18},{18,26},{... | collective-permute-start | bytes 259208 | tf_op jit(solution)/shard_map/ppermute | solution.py:29
  89.4 19.3 %collective-permute-start.32 = (f32[5,3,1440]{2,1,0:T(4,128)S(1)}, f32[5,3,1440]{2,1,0:T(4,128)S(1)}, u32[]{:S(2)}, u32[]{:S(2)}) collective-permute-start(f32[5,3,1440]{2,1,0:T(4,128)S(1)} %get-tuple-element.55), channel_id=1, source_target_pairs={{0,8},{8,16},{16,24},{1,9},{9,17},{17,25},{2,10},{10,18},{18,26},{... | collective-permute-start | bytes 259208 | tf_op jit(solution)/shard_map/ppermute | solution.py:29
  102.3 24.2 %collective-permute-start.11 = (f32[5,8,1440]{2,1,0:T(8,128)}, f32[5,8,1440]{2,1,0:T(8,128)S(1)}, u32[]{:S(2)}, u32[]{:S(2)}) collective-permute-start(f32[5,8,1440]{2,1,0:T(8,128)} %merid.8.refs_0_), channel_id=1, source_target_pairs={{0,1},{1,0},{2,3},{3,2},{4,5},{5,4},{6,7},{7,6},{8,9},{9,8},{10,11... | collective-permute-start | bytes 691208 | tf_op jit(solution)/shard_map/ppermute | solution.py:21
  105.7 23.1 %collective-permute-start.22 = (f32[5,8,1440]{2,1,0:T(8,128)}, f32[5,8,1440]{2,1,0:T(8,128)S(1)}, u32[]{:S(2)}, u32[]{:S(2)}) collective-permute-start(f32[5,8,1440]{2,1,0:T(8,128)} %merid.10.refs_0_), channel_id=1, source_target_pairs={{0,4},{1,5},{2,6},{3,7},{4,0},{5,1},{6,2},{7,3},{8,12},{9,13},{10,... | collective-permute-start | bytes 691208 | tf_op jit(solution)/shard_map/ppermute | solution.py:21
  126.5 20.5 %collective-permute-start.46 = (f32[5,8,1440]{2,1,0:T(8,128)}, f32[5,8,1440]{2,1,0:T(8,128)S(1)}, u32[]{:S(2)}, u32[]{:S(2)}) collective-permute-start(f32[5,8,1440]{2,1,0:T(8,128)} %merid.14.refs_0_), channel_id=1, source_target_pairs={{0,4},{1,5},{2,6},{3,7},{4,0},{5,1},{6,2},{7,3},{8,12},{9,13},{10,... | collective-permute-start | bytes 691208 | tf_op jit(solution)/shard_map/ppermute | solution.py:21
  131.5 26.1 %collective-permute-start.13 = (f32[5,8,1536]{2,1,0:T(8,128)S(1)}, f32[5,8,1536]{2,1,0:T(8,128)S(1)}, u32[]{:S(2)}, u32[]{:S(2)}) collective-permute-start(f32[5,8,1536]{2,1,0:T(8,128)S(1)} %get-tuple-element.21), channel_id=1, source_target_pairs={{0,2},{1,3},{2,0},{3,1},{4,6},{5,7},{6,4},{7,5},{8,10},{9,11},{10,... | collective-permute-start | bytes 737288 | tf_op jit(solution)/shard_map/ppermute | solution.py:21
  152.9 25.8 %collective-permute-start.37 = (f32[5,8,1536]{2,1,0:T(8,128)S(1)}, f32[5,8,1536]{2,1,0:T(8,128)S(1)}, u32[]{:S(2)}, u32[]{:S(2)}) collective-permute-start(f32[5,8,1536]{2,1,0:T(8,128)S(1)} %get-tuple-element.29), channel_id=1, source_target_pairs={{0,2},{1,3},{2,0},{3,1},{4,6},{5,7},{6,4},{7,5},{8,10},{9,11},{10,... | collective-permute-start | bytes 737288 | tf_op jit(solution)/shard_map/ppermute | solution.py:21
  157.6 26.2 %collective-permute-start.49 = (f32[5,8,1536]{2,1,0:T(8,128)S(1)}, f32[5,8,1536]{2,1,0:T(8,128)S(1)}, u32[]{:S(2)}, u32[]{:S(2)}) collective-permute-start(f32[5,8,1536]{2,1,0:T(8,128)S(1)} %get-tuple-element.33), channel_id=1, source_target_pairs={{0,2},{1,3},{2,0},{3,1},{4,6},{5,7},{6,4},{7,5},{8,10},{9,11},{10,... | collective-permute-start | bytes 737288 | tf_op jit(solution)/shard_map/ppermute | solution.py:21
  162.1 29.9 %collective-permute-start.14 = (f32[5,3,1440]{2,1,0:T(4,128)S(1)}, f32[5,3,1440]{2,1,0:T(4,128)S(1)}, u32[]{:S(2)}, u32[]{:S(2)}) collective-permute-start(f32[5,3,1440]{2,1,0:T(4,128)S(1)} %get-tuple-element.45), channel_id=1, source_target_pairs={{0,8},{8,16},{16,24},{1,9},{9,17},{17,25},{2,10},{10,18},{18,26},{... | collective-permute-start | bytes 259208 | tf_op jit(solution)/shard_map/ppermute | solution.py:29
  167.2 27.1 %collective-permute-start.15 = (f32[5,3,1440]{2,1,0:T(4,128)S(1)}, f32[5,3,1440]{2,1,0:T(4,128)S(1)}, u32[]{:S(2)}, u32[]{:S(2)}) collective-permute-start(f32[5,3,1440]{2,1,0:T(4,128)S(1)} %get-tuple-element.44), channel_id=1, source_target_pairs={{8,0},{16,8},{24,16},{9,1},{17,9},{25,17},{10,2},{18,10},{26,18},{... | collective-permute-start | bytes 259208 | tf_op jit(solution)/shard_map/ppermute | solution.py:30
  173.2 26.6 %collective-permute-start.26 = (f32[5,3,1440]{2,1,0:T(4,128)S(1)}, f32[5,3,1440]{2,1,0:T(4,128)S(1)}, u32[]{:S(2)}, u32[]{:S(2)}) collective-permute-start(f32[5,3,1440]{2,1,0:T(4,128)S(1)} %get-tuple-element.49), channel_id=1, source_target_pairs={{0,8},{8,16},{16,24},{1,9},{9,17},{17,25},{2,10},{10,18},{18,26},{... | collective-permute-start | bytes 259208 | tf_op jit(solution)/shard_map/ppermute | solution.py:29
  178.7 25.1 %collective-permute-start.27 = (f32[5,3,1440]{2,1,0:T(4,128)S(1)}, f32[5,3,1440]{2,1,0:T(4,128)S(1)}, u32[]{:S(2)}, u32[]{:S(2)}) collective-permute-start(f32[5,3,1440]{2,1,0:T(4,128)S(1)} %get-tuple-element.48), channel_id=1, source_target_pairs={{8,0},{16,8},{24,16},{9,1},{17,9},{25,17},{10,2},{18,10},{26,18},{... | collective-permute-start | bytes 259208 | tf_op jit(solution)/shard_map/ppermute | solution.py:30
  183.8 23.3 %collective-permute-start.38 = (f32[5,3,1440]{2,1,0:T(4,128)S(1)}, f32[5,3,1440]{2,1,0:T(4,128)S(1)}, u32[]{:S(2)}, u32[]{:S(2)}) collective-permute-start(f32[5,3,1440]{2,1,0:T(4,128)S(1)} %get-tuple-element.53), channel_id=1, source_target_pairs={{0,8},{8,16},{16,24},{1,9},{9,17},{17,25},{2,10},{10,18},{18,26},{... | collective-permute-start | bytes 259208 | tf_op jit(solution)/shard_map/ppermute | solution.py:29
  (73 other events, 485.7 us)

commit v2 on v1

--- a/solution.py
+++ b/solution.py
@@ -113,57 +113,128 @@
     )(plan, *own, *other)
 
 
-def zonal_kernel(mine, theirs, frac, out):
-    comps, band, width = out.shape
-    full = mine.shape[2]
-    fraction = frac[...]
-    for c in range(comps):
-        w = mine[c] + theirs[c]
-        w_1 = pltpu.roll(w, 1, 1)
-        w_2 = pltpu.roll(w, 2, 1)
-        w1 = pltpu.roll(w, full - 1, 1)
-        face = (7.0 * (w_1 + w) - (w_2 + w1)) / 12.0
-        flux = right_amount(w_1, pltpu.roll(face, 1, 1), face, fraction)
-        new = w + flux - pltpu.roll(flux, full - 1, 1)
-        out[c] = pltpu.roll(new, full - HALO, 1)[:, :width]
-
-
-def zonal(mine, theirs, frac, width):
-    comps, band, _ = mine.shape
+def stencil_kernel(levels, rows, *refs):
+    mine = refs[:levels]
+    theirs = refs[levels : 2 * levels]
+    frac, courant = refs[2 * levels : 2 * levels + 2]
+    out = refs[2 * levels + 2 : 3 * levels + 2]
+    to_north, to_south, south, north, send_sem, recv_sem = refs[3 * levels + 2 :]
+    comps, band, width = out[0].shape
+    full = mine[0].shape[2]
+    count = lax.axis_size("lat")
+    me = lax.axis_index("lat")
+    has_south = me > 0
+    has_north = me < count - 1
+    used = comps * HALO
+
+    barrier = pltpu.get_barrier_semaphore()
+
+    def greet(step):
+        pl.semaphore_signal(
+            barrier, inc=1, device_id={"lat": me + step}, device_id_type=pl.DeviceIdType.MESH
+        )
+
+    pl.when(has_south)(lambda: greet(-1))
+    pl.when(has_north)(lambda: greet(1))
+
+    def northward_copy(l):
+        return pltpu.make_async_remote_copy(
+            src_ref=to_north.at[l], dst_ref=south.at[l],
+            send_sem=send_sem.at[0, l], recv_sem=recv_sem.at[0, l],
+            device_id={"lat": me + 1}, device_id_type=pl.DeviceIdType.MESH,
+        )
+
+    def southward_copy(l):
+        return pltpu.make_async_remote_copy(
+            src_ref=to_south.at[l], dst_ref=north.at[l],
+            send_sem=send_sem.at[1, l], recv_sem=recv_sem.at[1, l],
+            device_id={"lat": me - 1}, device_id_type=pl.DeviceIdType.MESH,
+        )
+
+    @pl.when(me == 0)
+    def _():
+        south[...] = jnp.zeros_like(south)
+
+    @pl.when(me == count - 1)
+    def _():
+        north[...] = jnp.zeros_like(north)
+
+    for l in range(levels):
+        fraction = frac[l]
+        for c in range(comps):
+            w = mine[l][c] + theirs[l][c]
+            w_1 = pltpu.roll(w, 1, 1)
+            w_2 = pltpu.roll(w, 2, 1)
+            w1 = pltpu.roll(w, full - 1, 1)
+            face = (7.0 * (w_1 + w) - (w_2 + w1)) * (1.0 / 12.0)
+            flux = right_amount(w_1, pltpu.roll(face, 1, 1), face, fraction)
+            new = w + flux - pltpu.roll(flux, full - 1, 1)
+            new = pltpu.roll(new, full - HALO, 1)[:, :width]
+            out[l][c] = new
+            to_north[l, c * HALO : (c + 1) * HALO] = new[band - HALO :]
+            to_south[l, c * HALO : (c + 1) * HALO] = new[:HALO]
+        if rows > used:
+            pad = jnp.zeros((rows - used, width), jnp.float32)
+            to_north[l, used:rows] = pad
+            to_south[l, used:rows] = pad
+        if l == 0:
+            peers = has_south.astype(jnp.int32) + has_north.astype(jnp.int32)
+            pl.semaphore_wait(barrier, peers)
+        pl.when(has_north)(lambda l=l: northward_copy(l).start())
+        pl.when(has_south)(lambda l=l: southward_copy(l).start())
+
+    step = 2 * LANES
+    for l in range(levels):
+        pl.when(has_south)(lambda l=l: northward_copy(l).wait_recv())
+        pl.when(has_north)(lambda l=l: southward_copy(l).wait_recv())
+        for at in range(0, width, step):
+            cols = slice(at, min(at + step, width))
+            g = courant[l, HALO : HALO + band + 1, cols]
+            northward = jnp.maximum(g, 0.0)
+            southward = jnp.maximum(-g, 0.0)
+            for c in range(comps):
+                ends = slice(c * HALO, (c + 1) * HALO)
+                padded = jnp.concatenate(
+                    [south[l, ends, cols], out[l][c, :, cols], north[l, ends, cols]], axis=0
+                )
+                faces = (
+                    7.0 * (padded[1:-2] + padded[2:-1]) - (padded[:-3] + padded[3:])
+                ) * (1.0 / 12.0)
+                flux = right_amount(
+                    padded[2 : band + 3], faces[0 : band + 1], faces[1 : band + 2], northward
+                ) - left_amount(
+                    padded[3 : band + 4], faces[1 : band + 2], faces[2 : band + 3], southward
+                )
+                out[l][c, :, cols] = padded[3 : band + 3] + flux[:band] - flux[1:]
+
+    for l in range(levels):
+        pl.when(has_north)(lambda l=l: northward_copy(l).wait_send())
+        pl.when(has_south)(lambda l=l: southward_copy(l).wait_send())
+
+
+def stencils(mine, theirs, frac, courant, width, step):
+    levels = len(mine)
+    comps, band, _ = mine[0].shape
+    rows = round_up(comps * HALO, 8)
+    shape = jax.ShapeDtypeStruct((comps, band, width), jnp.float32)
+    vmem = pl.BlockSpec(memory_space=pltpu.VMEM)
+    halo = pltpu.VMEM((levels, rows, width), jnp.float32)
     return pl.pallas_call(
-        zonal_kernel,
-        out_shape=jax.ShapeDtypeStruct((comps, band, width), jnp.float32),
-        cost_estimate=pl.CostEstimate(flops=2_000_000, bytes_accessed=1_000_000, transcendentals=0),
-        name="zonal",
-    )(mine, theirs, frac)
-
-
-def merid_kernel(fields, south, north, courant, out):
-    comps, band, width = out.shape
-    step = 2 * LANES
-    for at in range(0, width, step):
-        cols = slice(at, min(at + step, width))
-        g = courant[HALO : HALO + band + 1, cols]
-        northward = jnp.maximum(g, 0.0)
-        southward = jnp.maximum(-g, 0.0)
-        for c in range(comps):
-            padded = jnp.concatenate([south[c, :, cols], fields[c, :, cols], north[c, :, cols]], axis=0)
-            faces = (7.0 * (padded[1:-2] + padded[2:-1]) - (padded[:-3] + padded[3:])) / 12.0
-            flux = right_amount(
-                padded[2 : band + 3], faces[0 : band + 1], faces[1 : band + 2], northward
-            ) - left_amount(
-                padded[3 : band + 4], faces[1 : band + 2], faces[2 : band + 3], southward
-            )
-            out[c, :, cols] = padded[3 : band + 3] + flux[:band] - flux[1:]
-
-
-def merid(fields, south, north, courant):
-    return pl.pallas_call(
-        merid_kernel,
-        out_shape=jax.ShapeDtypeStruct(fields.shape, jnp.float32),
-        cost_estimate=pl.CostEstimate(flops=4_000_000, bytes_accessed=1_000_000, transcendentals=0),
-        name="merid",
-    )(fields, south, north, courant)
+        functools.partial(stencil_kernel, levels, rows),
+        out_shape=(shape,) * levels,
+        in_specs=[vmem] * (2 * levels + 2),
+        out_specs=(vmem,) * levels,
+        scratch_shapes=[
+            halo, halo, halo, halo,
+            pltpu.SemaphoreType.DMA((2, levels)),
+            pltpu.SemaphoreType.DMA((2, levels)),
+        ],
+        compiler_params=pltpu.CompilerParams(
+            vmem_limit_bytes=32 * 1024 * 1024, collective_id=step, has_side_effects=True
+        ),
+        cost_estimate=pl.CostEstimate(flops=20_000_000, bytes_accessed=5_000_000, transcendentals=0),
+        name="stencils",
+    )(*mine, *theirs, frac, courant)
 
 
 def make_plan(shift, width, count, me):
@@ -213,13 +284,13 @@
             for l in range(levels):
                 held[l] = held[l] + [exchange(x, stride) for x in held[l]]
             stride *= 2
+        mine, theirs = [], []
         for l in range(levels):
             other = [exchange(x, 1) for x in held[l]]
-            mine, theirs = cut_windows(held[l], other, plan[l])
-            theirs = exchange(theirs, 2)
-            moved = zonal(mine, theirs, frac[l], width)
-            south, north = lat_halos(moved, 1)
-            fields[l] = merid(moved, south, north, courant[l])
+            kept, sent = cut_windows(held[l], other, plan[l])
+            mine.append(kept)
+            theirs.append(exchange(sent, 2))
+        fields = stencils(mine, theirs, frac, courant, width, step)
     result = jnp.stack(fields, axis=1)
     return (result[0], result[1:])
 

time: 221 us -> 204 us (0.923); the launches traced: 218 us -> 203 us
  waiting for transfers between devices: 39 us -> 103 us
  starting transfers between devices: 91.6 us -> 32.9 us
  local copies, waits for them, and re-layouts: 25.1 us -> 7.06 us
    ppermute x32, waiting for transfers between devices: 38.9 us -> 102 us  [exchange(): return lax.ppermute(array, 'lon', [(i, i ^ stride) for i in range(count)])]
    ppermute x9 -> x1, starting transfers between devices: 45 us -> 3.47 us  [lat_halos(): lax.ppermute(lax.slice_in_dim(block, size - HALO, size, axis=dim), 'lat',...]
    unnamed x96 -> x18, local copies, waits for them, and re-layouts: 14.3 us -> 1.64 us
    ppermute x9 -> x1, starting transfers between devices: 12 us -> 1.29 us  [lat_halos(): lax.ppermute(lax.slice_in_dim(block, 0, HALO, axis=dim), 'lat', backward)]
    slice x9 -> x1, local copies, waits for them, and re-layouts: 7.79 us -> 0.01 us  [local(): kept, sent = cut_windows(held[l], other, plan[l])]
    ppermute x32, starting transfers between devices: 31 us -> 24.7 us  [exchange(): return lax.ppermute(array, 'lon', [(i, i ^ stride) for i in range(count)])]
    pallas_call x16 -> x2, Pallas kernels: 42.5 us -> 40.7 us  [stencils(): pl.pallas_call(functools.partial(stencil_kernel, levels, rows), out_shape...]
  transfers between devices with their start and end apart: 52 -> 36, of which waited for: 6 -> 15; matrix products, arithmetic and copies ran while one was open for 5% -> 2% of each run, Pallas kernels for 26% -> 8%
where the time goes in v2:
time: 204 us; the launch traced here: 203 us
  waiting for transfers between devices  103 us (50%)
  Pallas kernels  56.7 us (28%)
  starting transfers between devices  32.9 us (16%)
  local copies, waits for them, and re-layouts  7.06 us (3%)
  other arithmetic  2.05 us (1%)
    ppermute x32, waiting for transfers between devices, exchange(): return lax.ppermute(array, 'lon', [(i, i ^ stride) for i in range(count)])  102 us
    pallas_call x2, Pallas kernels, stencils(): pl.pallas_call(functools.partial(stencil_kernel, levels, rows), out_shape...  40.7 us
    ppermute x32, starting transfers between devices, exchange(): return lax.ppermute(array, 'lon', [(i, i ^ stride) for i in range(count)])  24.7 us
    pallas_call x8, Pallas kernels, cut_windows(): pl.pallas_call(functools.partial(window_kernel, held, lead, width), out_s...  16 us
  transfers between devices with their start and end apart: 36, of which 15 were waited for; matrix products, arithmetic and copies ran while one was open for 2% of the time, Pallas kernels for 8%

profile of v2, /device:TPU:0, one launch (start us, length us, event | category | flops | bytes accessed | tf_op | source)
XLA Modules:
  0.0 203.2 jit_solution(11999178676229356021)
XLA Ops:
  3.3 3.7 %collective-permute-start = (f32[5,8,1440]{2,1,0:T(8,128)S(1)}, f32[5,8,1440]{2,1,0:T(8,128)S(1)}, u32[]{:S(2)}, u32[]{:S(2)}) collective-permute-start(f32[5,8,1440]{2,1,0:T(8,128)S(1)} %pad_maximum_fusion.4.refs_0_), channel_id=1, source_target_pairs={{0,4},{1,5},{2,6},{3,7},{4,0},{5,1},{6,2},{7,3},{8,12},{9,13},{10,... | collective-permute-start | bytes 691208 | tf_op jit(solution)/shard_map/ppermute | solution.py:21
  10.8 2.7 %collective-permute-start.6 = (f32[5,8,1440]{2,1,0:T(8,128)S(1)}, f32[5,8,1440]{2,1,0:T(8,128)S(1)}, u32[]{:S(2)}, u32[]{:S(2)}) collective-permute-start(f32[5,8,1440]{2,1,0:T(8,128)S(1)} %pad_maximum_fusion.6.refs_0_), channel_id=1, source_target_pairs={{0,4},{1,5},{2,6},{3,7},{4,0},{5,1},{6,2},{7,3},{8,12},{9,13},{10,... | collective-permute-start | bytes 691208 | tf_op jit(solution)/shard_map/ppermute | solution.py:21
  13.5 16.2 %collective-permute-done.refs_1_ = f32[5,8,1440]{2,1,0:T(8,128)S(1)} collective-permute-done((f32[5,8,1440]{2,1,0:T(8,128)S(1)}, f32[5,8,1440]{2,1,0:T(8,128)S(1)}, u32[]{:S(2)}, u32[]{:S(2)}) %collective-permute-start) | collective-permute-done | bytes 230432 | tf_op jit(solution)/shard_map/ppermute | solution.py:21
  29.7 10.4 %collective-permute-done.3.refs_1_ = f32[5,8,1440]{2,1,0:T(8,128)S(1)} collective-permute-done((f32[5,8,1440]{2,1,0:T(8,128)S(1)}, f32[5,8,1440]{2,1,0:T(8,128)S(1)}, u32[]{:S(2)}, u32[]{:S(2)}) %collective-permute-start.3) | collective-permute-done | bytes 230432 | tf_op jit(solution)/shard_map/ppermute | solution.py:21
  40.8 4.6 %collective-permute-done.6.refs_1_ = f32[5,8,1440]{2,1,0:T(8,128)S(1)} collective-permute-done((f32[5,8,1440]{2,1,0:T(8,128)S(1)}, f32[5,8,1440]{2,1,0:T(8,128)S(1)}, u32[]{:S(2)}, u32[]{:S(2)}) %collective-permute-start.6) | collective-permute-done | bytes 230432 | tf_op jit(solution)/shard_map/ppermute | solution.py:21
  45.4 5.0 %collective-permute-done.9.refs_1_ = f32[5,8,1440]{2,1,0:T(8,128)S(1)} collective-permute-done((f32[5,8,1440]{2,1,0:T(8,128)S(1)}, f32[5,8,1440]{2,1,0:T(8,128)S(1)}, u32[]{:S(2)}, u32[]{:S(2)}) %collective-permute-start.9) | collective-permute-done | bytes 230432 | tf_op jit(solution)/shard_map/ppermute | solution.py:21
  50.5 3.5 %collective-permute-start.18 = (f32[4,3,1440]{2,1,0:T(4,128)}, f32[4,3,1440]{2,1,0:T(4,128)S(1)}, u32[]{:S(2)}, u32[]{:S(2)}) collective-permute-start(f32[4,3,1440]{2,1,0:T(4,128)} %get-tuple-element.56), channel_id=1, source_target_pairs={{0,8},{8,16},{16,24},{1,9},{9,17},{17,25},{2,10},{10,18},{18,26},{... | collective-permute-start | bytes 207368 | tf_op jit(solution)/shard_map/ppermute | solution.py:29
  59.3 3.4 %collective-permute-start.17 = (f32[4,8,3]{2,1,0:T(8,128)S(1)}, f32[4,8,3]{2,1,0:T(8,128)}, u32[]{:S(2)}, u32[]{:S(2)}) collective-permute-start(f32[4,8,3]{2,1,0:T(8,128)S(1)} %copy-done.5), channel_id=1, source_target_pairs={{1,0},{2,1},{3,2},{4,3},{5,4},{6,5},{7,6},{0,7},{9,8},{10,9},{11,1... | collective-permute-start | bytes 1160 | tf_op jit(solution)/shard_map/ppermute | solution.py:270
  66.8 2.1 %collective-permute-start.13 = (f32[5,8,1536]{2,1,0:T(8,128)S(1)}, f32[5,8,1536]{2,1,0:T(8,128)S(1)}, u32[]{:S(2)}, u32[]{:S(2)}) collective-permute-start(f32[5,8,1536]{2,1,0:T(8,128)S(1)} %get-tuple-element.31), channel_id=1, source_target_pairs={{0,2},{1,3},{2,0},{3,1},{4,6},{5,7},{6,4},{7,5},{8,10},{9,11},{10,... | collective-permute-start | bytes 737288 | tf_op jit(solution)/shard_map/ppermute | solution.py:21
  74.1 5.1 %collective-permute-done.13.refs_5_ = f32[5,8,1536]{2,1,0:T(8,128)S(1)} collective-permute-done((f32[5,8,1536]{2,1,0:T(8,128)S(1)}, f32[5,8,1536]{2,1,0:T(8,128)S(1)}, u32[]{:S(2)}, u32[]{:S(2)}) %collective-permute-start.13) | collective-permute-done | bytes 245792 | tf_op jit(solution)/shard_map/ppermute | solution.py:21
  79.2 5.3 %collective-permute-done.14.refs_6_ = f32[5,8,1536]{2,1,0:T(8,128)S(1)} collective-permute-done((f32[5,8,1536]{2,1,0:T(8,128)S(1)}, f32[5,8,1536]{2,1,0:T(8,128)S(1)}, u32[]{:S(2)}, u32[]{:S(2)}) %collective-permute-start.14) | collective-permute-done | bytes 245792 | tf_op jit(solution)/shard_map/ppermute | solution.py:21
  84.4 2.8 %collective-permute-done.15.refs_7_ = f32[5,8,1536]{2,1,0:T(8,128)S(1)} collective-permute-done((f32[5,8,1536]{2,1,0:T(8,128)S(1)}, f32[5,8,1536]{2,1,0:T(8,128)S(1)}, u32[]{:S(2)}, u32[]{:S(2)}) %collective-permute-start.15) | collective-permute-done | bytes 245792 | tf_op jit(solution)/shard_map/ppermute | solution.py:21
  87.2 20.8 %stencils.2 = (f32[5,8,1440]{2,1,0:T(8,128)S(1)}, f32[5,8,1440]{2,1,0:T(8,128)S(1)}, f32[5,8,1440]{2,1,0:T(8,128)S(1)}, f32[5,8,1440]{2,1,0:T(8,128)S(1)}) custom-call(f32[5,8,1536]{2,1,0:T(8,128)S(1)} %get-tuple-element.26.refs_0_, f32[5,8,1536]{2,1,0:T(8,128)S(1)} %get-tuple-element.27.refs_1_, f32[5,8,1536]{2,1,0:T(8,128)S(1)} %get-tuple-element.28.refs_2_, ...), custom_call_target="tpu_custom_call" | custom-call | flops 20000000 | bytes 5000000 | tf_op jit(solution)/shard_map/stencils/pallas_call | solution.py:222
  108.1 3.9 %collective-permute-start.20 = (f32[5,8,1440]{2,1,0:T(8,128)S(1)}, f32[5,8,1440]{2,1,0:T(8,128)S(1)}, u32[]{:S(2)}, u32[]{:S(2)}) collective-permute-start(f32[5,8,1440]{2,1,0:T(8,128)S(1)} %get-tuple-element.34.refs_0_), channel_id=1, source_target_pairs={{0,4},{1,5},{2,6},{3,7},{4,0},{5,1},{6,2},{7,3},{8,12},{9,13},{10,... | collective-permute-start | bytes 691208 | tf_op jit(solution)/shard_map/ppermute | solution.py:21
  112.1 2.8 %collective-permute-start.26 = (f32[5,8,1440]{2,1,0:T(8,128)S(1)}, f32[5,8,1440]{2,1,0:T(8,128)S(1)}, u32[]{:S(2)}, u32[]{:S(2)}) collective-permute-start(f32[5,8,1440]{2,1,0:T(8,128)S(1)} %get-tuple-element.38.refs_0_), channel_id=1, source_target_pairs={{0,4},{1,5},{2,6},{3,7},{4,0},{5,1},{6,2},{7,3},{8,12},{9,13},{10,... | collective-permute-start | bytes 691208 | tf_op jit(solution)/shard_map/ppermute | solution.py:21
  115.1 24.7 %collective-permute-done.20.refs_1_ = f32[5,8,1440]{2,1,0:T(8,128)S(1)} collective-permute-done((f32[5,8,1440]{2,1,0:T(8,128)S(1)}, f32[5,8,1440]{2,1,0:T(8,128)S(1)}, u32[]{:S(2)}, u32[]{:S(2)}) %collective-permute-start.20) | collective-permute-done | bytes 230432 | tf_op jit(solution)/shard_map/ppermute | solution.py:21
  139.7 5.3 %collective-permute-done.23.refs_1_ = f32[5,8,1440]{2,1,0:T(8,128)S(1)} collective-permute-done((f32[5,8,1440]{2,1,0:T(8,128)S(1)}, f32[5,8,1440]{2,1,0:T(8,128)S(1)}, u32[]{:S(2)}, u32[]{:S(2)}) %collective-permute-start.23) | collective-permute-done | bytes 230432 | tf_op jit(solution)/shard_map/ppermute | solution.py:21
  145.5 4.8 %collective-permute-done.26.refs_1_ = f32[5,8,1440]{2,1,0:T(8,128)S(1)} collective-permute-done((f32[5,8,1440]{2,1,0:T(8,128)S(1)}, f32[5,8,1440]{2,1,0:T(8,128)S(1)}, u32[]{:S(2)}, u32[]{:S(2)}) %collective-permute-start.26) | collective-permute-done | bytes 230432 | tf_op jit(solution)/shard_map/ppermute | solution.py:21
  150.3 5.1 %collective-permute-done.29.refs_1_ = f32[5,8,1440]{2,1,0:T(8,128)S(1)} collective-permute-done((f32[5,8,1440]{2,1,0:T(8,128)S(1)}, f32[5,8,1440]{2,1,0:T(8,128)S(1)}, u32[]{:S(2)}, u32[]{:S(2)}) %collective-permute-start.29) | collective-permute-done | bytes 230432 | tf_op jit(solution)/shard_map/ppermute | solution.py:21
  164.1 2.2 %cut_windows.15 = (f32[5,8,1536]{2,1,0:T(8,128)S(1)}, f32[5,8,1536]{2,1,0:T(8,128)S(1)}) custom-call(s32[5,8]{1,0:T(8,128)S(1)} %bitcast.59, f32[5,8,1440]{2,1,0:T(8,128)S(1)} %get-tuple-element.40.refs_0_, f32[5,8,1440]{2,1,0:T(8,128)S(1)} %collective-permute-done.29.refs_1_, f32[5,8,1440]{2,1,0:T(8,128)S(1)} %collective-permute-done.30.refs_2_, ...), custom_call_target="tpu_custom_call" | custom-call | flops 2000000 | bytes 2000000 | tf_op jit(solution)/shard_map/cut_windows/pallas_call | solution.py:103
  168.3 3.7 %collective-permute-done.33.refs_5_ = f32[5,8,1536]{2,1,0:T(8,128)S(1)} collective-permute-done((f32[5,8,1536]{2,1,0:T(8,128)S(1)}, f32[5,8,1536]{2,1,0:T(8,128)S(1)}, u32[]{:S(2)}, u32[]{:S(2)}) %collective-permute-start.33) | collective-permute-done | bytes 245792 | tf_op jit(solution)/shard_map/ppermute | solution.py:21
  172.0 5.3 %collective-permute-done.34.refs_6_ = f32[5,8,1536]{2,1,0:T(8,128)S(1)} collective-permute-done((f32[5,8,1536]{2,1,0:T(8,128)S(1)}, f32[5,8,1536]{2,1,0:T(8,128)S(1)}, u32[]{:S(2)}, u32[]{:S(2)}) %collective-permute-start.34) | collective-permute-done | bytes 245792 | tf_op jit(solution)/shard_map/ppermute | solution.py:21
  177.3 4.3 %collective-permute-done.35.refs_7_ = f32[5,8,1536]{2,1,0:T(8,128)S(1)} collective-permute-done((f32[5,8,1536]{2,1,0:T(8,128)S(1)}, f32[5,8,1536]{2,1,0:T(8,128)S(1)}, u32[]{:S(2)}, u32[]{:S(2)}) %collective-permute-start.35) | collective-permute-done | bytes 245792 | tf_op jit(solution)/shard_map/ppermute | solution.py:21
  181.6 20.0 %stencils.3 = (f32[5,8,1440]{2,1,0:T(8,128)S(1)}, f32[5,8,1440]{2,1,0:T(8,128)S(1)}, f32[5,8,1440]{2,1,0:T(8,128)S(1)}, f32[5,8,1440]{2,1,0:T(8,128)S(1)}) custom-call(f32[5,8,1536]{2,1,0:T(8,128)S(1)} %get-tuple-element.35.refs_0_, f32[5,8,1536]{2,1,0:T(8,128)S(1)} %get-tuple-element.37.refs_1_, f32[5,8,1536]{2,1,0:T(8,128)S(1)} %get-tuple-element.39.refs_2_, ...), custom_call_target="tpu_custom_call" | custom-call | flops 20000000 | bytes 5000000 | tf_op jit(solution)/shard_map/stencils/pallas_call | solution.py:222
  (96 shorter events, 35.0 us)
Async XLA Ops:
  3.3 26.3 %collective-permute-start = (f32[5,8,1440]{2,1,0:T(8,128)S(1)}, f32[5,8,1440]{2,1,0:T(8,128)S(1)}, u32[]{:S(2)}, u32[]{:S(2)}) collective-permute-start(f32[5,8,1440]{2,1,0:T(8,128)S(1)} %pad_maximum_fusion.4.refs_0_), channel_id=1, source_target_pairs={{0,4},{1,5},{2,6},{3,7},{4,0},{5,1},{6,2},{7,3},{8,12},{9,13},{10,... | collective-permute-start | bytes 691208 | tf_op jit(solution)/shard_map/ppermute | solution.py:21
  7.0 22.6 %collective-permute-start.4 = (f32[5,8,1440]{2,1,0:T(8,128)S(1)}, f32[5,8,1440]{2,1,0:T(8,128)S(1)}, u32[]{:S(2)}, u32[]{:S(2)}) collective-permute-start(f32[5,8,1440]{2,1,0:T(8,128)S(1)} %pad_maximum_fusion.5.refs_0_), channel_id=1, source_target_pairs={{0,1},{1,0},{2,3},{3,2},{4,5},{5,4},{6,7},{7,6},{8,9},{9,8},{10,11... | collective-permute-start | bytes 691208 | tf_op jit(solution)/shard_map/ppermute | solution.py:21
  7.3 32.9 %collective-permute-start.3 = (f32[5,8,1440]{2,1,0:T(8,128)S(1)}, f32[5,8,1440]{2,1,0:T(8,128)S(1)}, u32[]{:S(2)}, u32[]{:S(2)}) collective-permute-start(f32[5,8,1440]{2,1,0:T(8,128)S(1)} %pad_maximum_fusion.5.refs_0_), channel_id=1, source_target_pairs={{0,4},{1,5},{2,6},{3,7},{4,0},{5,1},{6,2},{7,3},{8,12},{9,13},{10,... | collective-permute-start | bytes 691208 | tf_op jit(solution)/shard_map/ppermute | solution.py:21
  7.6 32.6 %collective-permute-start.7 = (f32[5,8,1440]{2,1,0:T(8,128)S(1)}, f32[5,8,1440]{2,1,0:T(8,128)S(1)}, u32[]{:S(2)}, u32[]{:S(2)}) collective-permute-start(f32[5,8,1440]{2,1,0:T(8,128)S(1)} %pad_maximum_fusion.6.refs_0_), channel_id=1, source_target_pairs={{0,1},{1,0},{2,3},{3,2},{4,5},{5,4},{6,7},{7,6},{8,9},{9,8},{10,11... | collective-permute-start | bytes 691208 | tf_op jit(solution)/shard_map/ppermute | solution.py:21
  10.8 34.7 %collective-permute-start.6 = (f32[5,8,1440]{2,1,0:T(8,128)S(1)}, f32[5,8,1440]{2,1,0:T(8,128)S(1)}, u32[]{:S(2)}, u32[]{:S(2)}) collective-permute-start(f32[5,8,1440]{2,1,0:T(8,128)S(1)} %pad_maximum_fusion.6.refs_0_), channel_id=1, source_target_pairs={{0,4},{1,5},{2,6},{3,7},{4,0},{5,1},{6,2},{7,3},{8,12},{9,13},{10,... | collective-permute-start | bytes 691208 | tf_op jit(solution)/shard_map/ppermute | solution.py:21
  29.6 20.8 %collective-permute-start.9 = (f32[5,8,1440]{2,1,0:T(8,128)S(1)}, f32[5,8,1440]{2,1,0:T(8,128)S(1)}, u32[]{:S(2)}, u32[]{:S(2)}) collective-permute-start(f32[5,8,1440]{2,1,0:T(8,128)S(1)} %pad_maximum_fusion.7.refs_0_), channel_id=1, source_target_pairs={{0,4},{1,5},{2,6},{3,7},{4,0},{5,1},{6,2},{7,3},{8,12},{9,13},{10,... | collective-permute-start | bytes 691208 | tf_op jit(solution)/shard_map/ppermute | solution.py:21
  29.7 20.8 %collective-permute-start.2 = (f32[5,8,1440]{2,1,0:T(8,128)S(1)}, f32[5,8,1440]{2,1,0:T(8,128)S(1)}, u32[]{:S(2)}, u32[]{:S(2)}) collective-permute-start(f32[5,8,1440]{2,1,0:T(8,128)S(1)} %collective-permute-done.refs_1_), channel_id=1, source_target_pairs={{0,1},{1,0},{2,3},{3,2},{4,5},{5,4},{6,7},{7,6},{8,9},{9,8},{10,11... | collective-permute-start | bytes 691208 | tf_op jit(solution)/shard_map/ppermute | solution.py:21
  40.1 13.8 %collective-permute-start.5 = (f32[5,8,1440]{2,1,0:T(8,128)S(1)}, f32[5,8,1440]{2,1,0:T(8,128)S(1)}, u32[]{:S(2)}, u32[]{:S(2)}) collective-permute-start(f32[5,8,1440]{2,1,0:T(8,128)S(1)} %collective-permute-done.3.refs_1_), channel_id=1, source_target_pairs={{0,1},{1,0},{2,3},{3,2},{4,5},{5,4},{6,7},{7,6},{8,9},{9,8},{10,11... | collective-permute-start | bytes 691208 | tf_op jit(solution)/shard_map/ppermute | solution.py:21
  40.2 24.5 %collective-permute-start.10 = (f32[5,8,1440]{2,1,0:T(8,128)S(1)}, f32[5,8,1440]{2,1,0:T(8,128)S(1)}, u32[]{:S(2)}, u32[]{:S(2)}) collective-permute-start(f32[5,8,1440]{2,1,0:T(8,128)S(1)} %pad_maximum_fusion.7.refs_0_), channel_id=1, source_target_pairs={{0,1},{1,0},{2,3},{3,2},{4,5},{5,4},{6,7},{7,6},{8,9},{9,8},{10,11... | collective-permute-start | bytes 691208 | tf_op jit(solution)/shard_map/ppermute | solution.py:21
  45.4 13.9 %collective-permute-start.8 = (f32[5,8,1440]{2,1,0:T(8,128)S(1)}, f32[5,8,1440]{2,1,0:T(8,128)S(1)}, u32[]{:S(2)}, u32[]{:S(2)}) collective-permute-start(f32[5,8,1440]{2,1,0:T(8,128)S(1)} %collective-permute-done.6.refs_1_), channel_id=1, source_target_pairs={{0,1},{1,0},{2,3},{3,2},{4,5},{5,4},{6,7},{7,6},{8,9},{9,8},{10,11... | collective-permute-start | bytes 691208 | tf_op jit(solution)/shard_map/ppermute | solution.py:21
  50.4 14.3 %collective-permute-start.11 = (f32[5,8,1440]{2,1,0:T(8,128)S(1)}, f32[5,8,1440]{2,1,0:T(8,128)S(1)}, u32[]{:S(2)}, u32[]{:S(2)}) collective-permute-start(f32[5,8,1440]{2,1,0:T(8,128)S(1)} %collective-permute-done.9.refs_1_), channel_id=1, source_target_pairs={{0,1},{1,0},{2,3},{3,2},{4,5},{5,4},{6,7},{7,6},{8,9},{9,8},{10,11... | collective-permute-start | bytes 691208 | tf_op jit(solution)/shard_map/ppermute | solution.py:21
  50.5 19.5 %collective-permute-start.18 = (f32[4,3,1440]{2,1,0:T(4,128)}, f32[4,3,1440]{2,1,0:T(4,128)S(1)}, u32[]{:S(2)}, u32[]{:S(2)}) collective-permute-start(f32[4,3,1440]{2,1,0:T(4,128)} %get-tuple-element.56), channel_id=1, source_target_pairs={{0,8},{8,16},{16,24},{1,9},{9,17},{17,25},{2,10},{10,18},{18,26},{... | collective-permute-start | bytes 207368 | tf_op jit(solution)/shard_map/ppermute | solution.py:29
  54.0 19.1 %collective-permute-start.19 = (f32[4,3,1440]{2,1,0:T(4,128)}, f32[4,3,1440]{2,1,0:T(4,128)}, u32[]{:S(2)}, u32[]{:S(2)}) collective-permute-start(f32[4,3,1440]{2,1,0:T(4,128)} %get-tuple-element.57), channel_id=1, source_target_pairs={{8,0},{16,8},{24,16},{9,1},{17,9},{25,17},{10,2},{18,10},{26,18},{... | collective-permute-start | bytes 207368 | tf_op jit(solution)/shard_map/ppermute | solution.py:30
  69.9 14.5 %collective-permute-start.14 = (f32[5,8,1536]{2,1,0:T(8,128)S(1)}, f32[5,8,1536]{2,1,0:T(8,128)S(1)}, u32[]{:S(2)}, u32[]{:S(2)}) collective-permute-start(f32[5,8,1536]{2,1,0:T(8,128)S(1)} %get-tuple-element.32), channel_id=1, source_target_pairs={{0,2},{1,3},{2,0},{3,1},{4,6},{5,7},{6,4},{7,5},{8,10},{9,11},{10,... | collective-permute-start | bytes 737288 | tf_op jit(solution)/shard_map/ppermute | solution.py:21
  69.9 17.3 %collective-permute-start.15 = (f32[5,8,1536]{2,1,0:T(8,128)S(1)}, f32[5,8,1536]{2,1,0:T(8,128)S(1)}, u32[]{:S(2)}, u32[]{:S(2)}) collective-permute-start(f32[5,8,1536]{2,1,0:T(8,128)S(1)} %get-tuple-element.33), channel_id=1, source_target_pairs={{0,2},{1,3},{2,0},{3,1},{4,6},{5,7},{6,4},{7,5},{8,10},{9,11},{10,... | collective-permute-start | bytes 737288 | tf_op jit(solution)/shard_map/ppermute | solution.py:21
  108.1 31.6 %collective-permute-start.20 = (f32[5,8,1440]{2,1,0:T(8,128)S(1)}, f32[5,8,1440]{2,1,0:T(8,128)S(1)}, u32[]{:S(2)}, u32[]{:S(2)}) collective-permute-start(f32[5,8,1440]{2,1,0:T(8,128)S(1)} %get-tuple-element.34.refs_0_), channel_id=1, source_target_pairs={{0,4},{1,5},{2,6},{3,7},{4,0},{5,1},{6,2},{7,3},{8,12},{9,13},{10,... | collective-permute-start | bytes 691208 | tf_op jit(solution)/shard_map/ppermute | solution.py:21
  112.0 33.0 %collective-permute-start.23 = (f32[5,8,1440]{2,1,0:T(8,128)S(1)}, f32[5,8,1440]{2,1,0:T(8,128)S(1)}, u32[]{:S(2)}, u32[]{:S(2)}) collective-permute-start(f32[5,8,1440]{2,1,0:T(8,128)S(1)} %get-tuple-element.36.refs_0_), channel_id=1, source_target_pairs={{0,4},{1,5},{2,6},{3,7},{4,0},{5,1},{6,2},{7,3},{8,12},{9,13},{10,... | collective-permute-start | bytes 691208 | tf_op jit(solution)/shard_map/ppermute | solution.py:21
  112.0 33.0 %collective-permute-start.24 = (f32[5,8,1440]{2,1,0:T(8,128)S(1)}, f32[5,8,1440]{2,1,0:T(8,128)S(1)}, u32[]{:S(2)}, u32[]{:S(2)}) collective-permute-start(f32[5,8,1440]{2,1,0:T(8,128)S(1)} %get-tuple-element.36.refs_0_), channel_id=1, source_target_pairs={{0,1},{1,0},{2,3},{3,2},{4,5},{5,4},{6,7},{7,6},{8,9},{9,8},{10,11... | collective-permute-start | bytes 691208 | tf_op jit(solution)/shard_map/ppermute | solution.py:21
  112.1 38.2 %collective-permute-start.26 = (f32[5,8,1440]{2,1,0:T(8,128)S(1)}, f32[5,8,1440]{2,1,0:T(8,128)S(1)}, u32[]{:S(2)}, u32[]{:S(2)}) collective-permute-start(f32[5,8,1440]{2,1,0:T(8,128)S(1)} %get-tuple-element.38.refs_0_), channel_id=1, source_target_pairs={{0,4},{1,5},{2,6},{3,7},{4,0},{5,1},{6,2},{7,3},{8,12},{9,13},{10,... | collective-permute-start | bytes 691208 | tf_op jit(solution)/shard_map/ppermute | solution.py:21
  114.9 40.4 %collective-permute-start.29 = (f32[5,8,1440]{2,1,0:T(8,128)S(1)}, f32[5,8,1440]{2,1,0:T(8,128)S(1)}, u32[]{:S(2)}, u32[]{:S(2)}) collective-permute-start(f32[5,8,1440]{2,1,0:T(8,128)S(1)} %get-tuple-element.40.refs_0_), channel_id=1, source_target_pairs={{0,4},{1,5},{2,6},{3,7},{4,0},{5,1},{6,2},{7,3},{8,12},{9,13},{10,... | collective-permute-start | bytes 691208 | tf_op jit(solution)/shard_map/ppermute | solution.py:21
  139.7 15.6 %collective-permute-start.22 = (f32[5,8,1440]{2,1,0:T(8,128)S(1)}, f32[5,8,1440]{2,1,0:T(8,128)S(1)}, u32[]{:S(2)}, u32[]{:S(2)}) collective-permute-start(f32[5,8,1440]{2,1,0:T(8,128)S(1)} %collective-permute-done.20.refs_1_), channel_id=1, source_target_pairs={{0,1},{1,0},{2,3},{3,2},{4,5},{5,4},{6,7},{7,6},{8,9},{9,8},{10,11... | collective-permute-start | bytes 691208 | tf_op jit(solution)/shard_map/ppermute | solution.py:21
  145.0 14.9 %collective-permute-start.27 = (f32[5,8,1440]{2,1,0:T(8,128)S(1)}, f32[5,8,1440]{2,1,0:T(8,128)S(1)}, u32[]{:S(2)}, u32[]{:S(2)}) collective-permute-start(f32[5,8,1440]{2,1,0:T(8,128)S(1)} %get-tuple-element.38.refs_0_), channel_id=1, source_target_pairs={{0,1},{1,0},{2,3},{3,2},{4,5},{5,4},{6,7},{7,6},{8,9},{9,8},{10,11... | collective-permute-start | bytes 691208 | tf_op jit(solution)/shard_map/ppermute | solution.py:21
  164.0 13.3 %collective-permute-start.34 = (f32[5,8,1536]{2,1,0:T(8,128)S(1)}, f32[5,8,1536]{2,1,0:T(8,128)S(1)}, u32[]{:S(2)}, u32[]{:S(2)}) collective-permute-start(f32[5,8,1536]{2,1,0:T(8,128)S(1)} %get-tuple-element.44), channel_id=1, source_target_pairs={{0,2},{1,3},{2,0},{3,1},{4,6},{5,7},{6,4},{7,5},{8,10},{9,11},{10,... | collective-permute-start | bytes 737288 | tf_op jit(solution)/shard_map/ppermute | solution.py:21
  166.3 15.3 %collective-permute-start.35 = (f32[5,8,1536]{2,1,0:T(8,128)S(1)}, f32[5,8,1536]{2,1,0:T(8,128)S(1)}, u32[]{:S(2)}, u32[]{:S(2)}) collective-permute-start(f32[5,8,1536]{2,1,0:T(8,128)S(1)} %get-tuple-element.45), channel_id=1, source_target_pairs={{0,2},{1,3},{2,0},{3,1},{4,6},{5,7},{6,4},{7,5},{8,10},{9,11},{10,... | collective-permute-start | bytes 737288 | tf_op jit(solution)/shard_map/ppermute | solution.py:21
  (18 other events, 121.9 us)

commit v3 on v2

--- a/solution.py
+++ b/solution.py
@@ -36,14 +36,6 @@
     curve = 6.0 * centre - 3.0 * (left_edge + right_edge)
     return fraction * (
         right_edge - 0.5 * fraction * (slope - (1.0 - fraction * (2.0 / 3.0)) * curve)
-    )
-
-
-def left_amount(centre, left_edge, right_edge, fraction):
-    slope = right_edge - left_edge
-    curve = 6.0 * centre - 3.0 * (left_edge + right_edge)
-    return fraction * (
-        left_edge + 0.5 * fraction * (slope + (1.0 - fraction * (2.0 / 3.0)) * curve)
     )
 
 
@@ -190,8 +182,10 @@
         for at in range(0, width, step):
             cols = slice(at, min(at + step, width))
             g = courant[l, HALO : HALO + band + 1, cols]
-            northward = jnp.maximum(g, 0.0)
-            southward = jnp.maximum(-g, 0.0)
+            half = 0.5 * g * g
+            rest = 1.0 - jnp.abs(g) * (2.0 / 3.0)
+            north_going = g > 0.0
+            rest = jnp.where(north_going, rest, -rest)
             for c in range(comps):
                 ends = slice(c * HALO, (c + 1) * HALO)
                 padded = jnp.concatenate(
@@ -200,11 +194,11 @@
                 faces = (
                     7.0 * (padded[1:-2] + padded[2:-1]) - (padded[:-3] + padded[3:])
                 ) * (1.0 / 12.0)
-                flux = right_amount(
-                    padded[2 : band + 3], faces[0 : band + 1], faces[1 : band + 2], northward
-                ) - left_amount(
-                    padded[3 : band + 4], faces[1 : band + 2], faces[2 : band + 3], southward
-                )
+                slope = faces[1:] - faces[:-1]
+                curve = 6.0 * padded[2 : band + 4] - 3.0 * (faces[1:] + faces[:-1])
+                slope = jnp.where(north_going, slope[:-1], slope[1:])
+                curve = jnp.where(north_going, curve[:-1], curve[1:])
+                flux = g * faces[1 : band + 2] - half * (slope - rest * curve)
                 out[l][c, :, cols] = padded[3 : band + 3] + flux[:band] - flux[1:]
 
     for l in range(levels):

time: 204 us -> 203 us (level)
  no operation moved by 1% of the time
where the time goes in v3:
time: 203 us
  waiting for transfers between devices  104 us (51%)
  Pallas kernels  56 us (28%)
  starting transfers between devices  32.9 us (16%)
  local copies, waits for them, and re-layouts  7.06 us (3%)
  other arithmetic  2.05 us (1%)
    ppermute x32, waiting for transfers between devices, exchange(): return lax.ppermute(array, 'lon', [(i, i ^ stride) for i in range(count)])  103 us
    pallas_call x2, Pallas kernels, stencils(): pl.pallas_call(functools.partial(stencil_kernel, levels, rows), out_shape...  40.2 us
    ppermute x32, starting transfers between devices, exchange(): return lax.ppermute(array, 'lon', [(i, i ^ stride) for i in range(count)])  24.7 us
    pallas_call x8, Pallas kernels, cut_windows(): pl.pallas_call(functools.partial(window_kernel, held, lead, width), out_s...  15.8 us
  transfers between devices with their start and end apart: 36, of which 15 were waited for; matrix products, arithmetic and copies ran while one was open for 2% of the time, Pallas kernels for 8%

profile of v3, /device:TPU:0, one launch (start us, length us, event | category | flops | bytes accessed | tf_op | source)
XLA Modules:
  0.0 202.7 jit_solution(5082525551897389502)
XLA Ops:
  3.3 3.7 %collective-permute-start = (f32[5,8,1440]{2,1,0:T(8,128)S(1)}, f32[5,8,1440]{2,1,0:T(8,128)S(1)}, u32[]{:S(2)}, u32[]{:S(2)}) collective-permute-start(f32[5,8,1440]{2,1,0:T(8,128)S(1)} %pad_maximum_fusion.4.refs_0_), channel_id=1, source_target_pairs={{0,4},{1,5},{2,6},{3,7},{4,0},{5,1},{6,2},{7,3},{8,12},{9,13},{10,... | collective-permute-start | bytes 691208 | tf_op jit(solution)/shard_map/ppermute | solution.py:21
  10.8 2.7 %collective-permute-start.6 = (f32[5,8,1440]{2,1,0:T(8,128)S(1)}, f32[5,8,1440]{2,1,0:T(8,128)S(1)}, u32[]{:S(2)}, u32[]{:S(2)}) collective-permute-start(f32[5,8,1440]{2,1,0:T(8,128)S(1)} %pad_maximum_fusion.6.refs_0_), channel_id=1, source_target_pairs={{0,4},{1,5},{2,6},{3,7},{4,0},{5,1},{6,2},{7,3},{8,12},{9,13},{10,... | collective-permute-start | bytes 691208 | tf_op jit(solution)/shard_map/ppermute | solution.py:21
  13.5 16.2 %collective-permute-done.refs_1_ = f32[5,8,1440]{2,1,0:T(8,128)S(1)} collective-permute-done((f32[5,8,1440]{2,1,0:T(8,128)S(1)}, f32[5,8,1440]{2,1,0:T(8,128)S(1)}, u32[]{:S(2)}, u32[]{:S(2)}) %collective-permute-start) | collective-permute-done | bytes 230432 | tf_op jit(solution)/shard_map/ppermute | solution.py:21
  29.7 10.4 %collective-permute-done.3.refs_1_ = f32[5,8,1440]{2,1,0:T(8,128)S(1)} collective-permute-done((f32[5,8,1440]{2,1,0:T(8,128)S(1)}, f32[5,8,1440]{2,1,0:T(8,128)S(1)}, u32[]{:S(2)}, u32[]{:S(2)}) %collective-permute-start.3) | collective-permute-done | bytes 230432 | tf_op jit(solution)/shard_map/ppermute | solution.py:21
  40.8 4.6 %collective-permute-done.6.refs_1_ = f32[5,8,1440]{2,1,0:T(8,128)S(1)} collective-permute-done((f32[5,8,1440]{2,1,0:T(8,128)S(1)}, f32[5,8,1440]{2,1,0:T(8,128)S(1)}, u32[]{:S(2)}, u32[]{:S(2)}) %collective-permute-start.6) | collective-permute-done | bytes 230432 | tf_op jit(solution)/shard_map/ppermute | solution.py:21
  45.4 5.0 %collective-permute-done.9.refs_1_ = f32[5,8,1440]{2,1,0:T(8,128)S(1)} collective-permute-done((f32[5,8,1440]{2,1,0:T(8,128)S(1)}, f32[5,8,1440]{2,1,0:T(8,128)S(1)}, u32[]{:S(2)}, u32[]{:S(2)}) %collective-permute-start.9) | collective-permute-done | bytes 230432 | tf_op jit(solution)/shard_map/ppermute | solution.py:21
  50.5 3.5 %collective-permute-start.18 = (f32[4,3,1440]{2,1,0:T(4,128)}, f32[4,3,1440]{2,1,0:T(4,128)S(1)}, u32[]{:S(2)}, u32[]{:S(2)}) collective-permute-start(f32[4,3,1440]{2,1,0:T(4,128)} %get-tuple-element.56), channel_id=1, source_target_pairs={{0,8},{8,16},{16,24},{1,9},{9,17},{17,25},{2,10},{10,18},{18,26},{... | collective-permute-start | bytes 207368 | tf_op jit(solution)/shard_map/ppermute | solution.py:29
  59.3 3.4 %collective-permute-start.17 = (f32[4,8,3]{2,1,0:T(8,128)S(1)}, f32[4,8,3]{2,1,0:T(8,128)}, u32[]{:S(2)}, u32[]{:S(2)}) collective-permute-start(f32[4,8,3]{2,1,0:T(8,128)S(1)} %copy-done.5), channel_id=1, source_target_pairs={{1,0},{2,1},{3,2},{4,3},{5,4},{6,5},{7,6},{0,7},{9,8},{10,9},{11,1... | collective-permute-start | bytes 1160 | tf_op jit(solution)/shard_map/ppermute | solution.py:264
  66.8 2.1 %collective-permute-start.13 = (f32[5,8,1536]{2,1,0:T(8,128)S(1)}, f32[5,8,1536]{2,1,0:T(8,128)S(1)}, u32[]{:S(2)}, u32[]{:S(2)}) collective-permute-start(f32[5,8,1536]{2,1,0:T(8,128)S(1)} %get-tuple-element.31), channel_id=1, source_target_pairs={{0,2},{1,3},{2,0},{3,1},{4,6},{5,7},{6,4},{7,5},{8,10},{9,11},{10,... | collective-permute-start | bytes 737288 | tf_op jit(solution)/shard_map/ppermute | solution.py:21
  74.1 5.1 %collective-permute-done.13.refs_5_ = f32[5,8,1536]{2,1,0:T(8,128)S(1)} collective-permute-done((f32[5,8,1536]{2,1,0:T(8,128)S(1)}, f32[5,8,1536]{2,1,0:T(8,128)S(1)}, u32[]{:S(2)}, u32[]{:S(2)}) %collective-permute-start.13) | collective-permute-done | bytes 245792 | tf_op jit(solution)/shard_map/ppermute | solution.py:21
  79.2 5.3 %collective-permute-done.14.refs_6_ = f32[5,8,1536]{2,1,0:T(8,128)S(1)} collective-permute-done((f32[5,8,1536]{2,1,0:T(8,128)S(1)}, f32[5,8,1536]{2,1,0:T(8,128)S(1)}, u32[]{:S(2)}, u32[]{:S(2)}) %collective-permute-start.14) | collective-permute-done | bytes 245792 | tf_op jit(solution)/shard_map/ppermute | solution.py:21
  84.4 2.8 %collective-permute-done.15.refs_7_ = f32[5,8,1536]{2,1,0:T(8,128)S(1)} collective-permute-done((f32[5,8,1536]{2,1,0:T(8,128)S(1)}, f32[5,8,1536]{2,1,0:T(8,128)S(1)}, u32[]{:S(2)}, u32[]{:S(2)}) %collective-permute-start.15) | collective-permute-done | bytes 245792 | tf_op jit(solution)/shard_map/ppermute | solution.py:21
  87.2 20.5 %stencils.2 = (f32[5,8,1440]{2,1,0:T(8,128)S(1)}, f32[5,8,1440]{2,1,0:T(8,128)S(1)}, f32[5,8,1440]{2,1,0:T(8,128)S(1)}, f32[5,8,1440]{2,1,0:T(8,128)S(1)}) custom-call(f32[5,8,1536]{2,1,0:T(8,128)S(1)} %get-tuple-element.26.refs_0_, f32[5,8,1536]{2,1,0:T(8,128)S(1)} %get-tuple-element.27.refs_1_, f32[5,8,1536]{2,1,0:T(8,128)S(1)} %get-tuple-element.28.refs_2_, ...), custom_call_target="tpu_custom_call" | custom-call | flops 20000000 | bytes 5000000 | tf_op jit(solution)/shard_map/stencils/pallas_call | solution.py:216
  107.9 3.9 %collective-permute-start.20 = (f32[5,8,1440]{2,1,0:T(8,128)S(1)}, f32[5,8,1440]{2,1,0:T(8,128)S(1)}, u32[]{:S(2)}, u32[]{:S(2)}) collective-permute-start(f32[5,8,1440]{2,1,0:T(8,128)S(1)} %get-tuple-element.34.refs_0_), channel_id=1, source_target_pairs={{0,4},{1,5},{2,6},{3,7},{4,0},{5,1},{6,2},{7,3},{8,12},{9,13},{10,... | collective-permute-start | bytes 691208 | tf_op jit(solution)/shard_map/ppermute | solution.py:21
  111.9 2.8 %collective-permute-start.26 = (f32[5,8,1440]{2,1,0:T(8,128)S(1)}, f32[5,8,1440]{2,1,0:T(8,128)S(1)}, u32[]{:S(2)}, u32[]{:S(2)}) collective-permute-start(f32[5,8,1440]{2,1,0:T(8,128)S(1)} %get-tuple-element.38.refs_0_), channel_id=1, source_target_pairs={{0,4},{1,5},{2,6},{3,7},{4,0},{5,1},{6,2},{7,3},{8,12},{9,13},{10,... | collective-permute-start | bytes 691208 | tf_op jit(solution)/shard_map/ppermute | solution.py:21
  114.8 24.7 %collective-permute-done.20.refs_1_ = f32[5,8,1440]{2,1,0:T(8,128)S(1)} collective-permute-done((f32[5,8,1440]{2,1,0:T(8,128)S(1)}, f32[5,8,1440]{2,1,0:T(8,128)S(1)}, u32[]{:S(2)}, u32[]{:S(2)}) %collective-permute-start.20) | collective-permute-done | bytes 230432 | tf_op jit(solution)/shard_map/ppermute | solution.py:21
  139.5 5.3 %collective-permute-done.23.refs_1_ = f32[5,8,1440]{2,1,0:T(8,128)S(1)} collective-permute-done((f32[5,8,1440]{2,1,0:T(8,128)S(1)}, f32[5,8,1440]{2,1,0:T(8,128)S(1)}, u32[]{:S(2)}, u32[]{:S(2)}) %collective-permute-start.23) | collective-permute-done | bytes 230432 | tf_op jit(solution)/shard_map/ppermute | solution.py:21
  145.3 4.8 %collective-permute-done.26.refs_1_ = f32[5,8,1440]{2,1,0:T(8,128)S(1)} collective-permute-done((f32[5,8,1440]{2,1,0:T(8,128)S(1)}, f32[5,8,1440]{2,1,0:T(8,128)S(1)}, u32[]{:S(2)}, u32[]{:S(2)}) %collective-permute-start.26) | collective-permute-done | bytes 230432 | tf_op jit(solution)/shard_map/ppermute | solution.py:21
  150.0 5.1 %collective-permute-done.29.refs_1_ = f32[5,8,1440]{2,1,0:T(8,128)S(1)} collective-permute-done((f32[5,8,1440]{2,1,0:T(8,128)S(1)}, f32[5,8,1440]{2,1,0:T(8,128)S(1)}, u32[]{:S(2)}, u32[]{:S(2)}) %collective-permute-start.29) | collective-permute-done | bytes 230432 | tf_op jit(solution)/shard_map/ppermute | solution.py:21
  159.7 2.1 %collective-permute-start.33 = (f32[5,8,1536]{2,1,0:T(8,128)S(1)}, f32[5,8,1536]{2,1,0:T(8,128)S(1)}, u32[]{:S(2)}, u32[]{:S(2)}) collective-permute-start(f32[5,8,1536]{2,1,0:T(8,128)S(1)} %get-tuple-element.43), channel_id=1, source_target_pairs={{0,2},{1,3},{2,0},{3,1},{4,6},{5,7},{6,4},{7,5},{8,10},{9,11},{10,... | collective-permute-start | bytes 737288 | tf_op jit(solution)/shard_map/ppermute | solution.py:21
  167.9 3.9 %collective-permute-done.33.refs_5_ = f32[5,8,1536]{2,1,0:T(8,128)S(1)} collective-permute-done((f32[5,8,1536]{2,1,0:T(8,128)S(1)}, f32[5,8,1536]{2,1,0:T(8,128)S(1)}, u32[]{:S(2)}, u32[]{:S(2)}) %collective-permute-start.33) | collective-permute-done | bytes 245792 | tf_op jit(solution)/shard_map/ppermute | solution.py:21
  171.7 5.3 %collective-permute-done.34.refs_6_ = f32[5,8,1536]{2,1,0:T(8,128)S(1)} collective-permute-done((f32[5,8,1536]{2,1,0:T(8,128)S(1)}, f32[5,8,1536]{2,1,0:T(8,128)S(1)}, u32[]{:S(2)}, u32[]{:S(2)}) %collective-permute-start.34) | collective-permute-done | bytes 245792 | tf_op jit(solution)/shard_map/ppermute | solution.py:21
  177.0 4.3 %collective-permute-done.35.refs_7_ = f32[5,8,1536]{2,1,0:T(8,128)S(1)} collective-permute-done((f32[5,8,1536]{2,1,0:T(8,128)S(1)}, f32[5,8,1536]{2,1,0:T(8,128)S(1)}, u32[]{:S(2)}, u32[]{:S(2)}) %collective-permute-start.35) | collective-permute-done | bytes 245792 | tf_op jit(solution)/shard_map/ppermute | solution.py:21
  181.3 19.7 %stencils.3 = (f32[5,8,1440]{2,1,0:T(8,128)S(1)}, f32[5,8,1440]{2,1,0:T(8,128)S(1)}, f32[5,8,1440]{2,1,0:T(8,128)S(1)}, f32[5,8,1440]{2,1,0:T(8,128)S(1)}) custom-call(f32[5,8,1536]{2,1,0:T(8,128)S(1)} %get-tuple-element.35.refs_0_, f32[5,8,1536]{2,1,0:T(8,128)S(1)} %get-tuple-element.37.refs_1_, f32[5,8,1536]{2,1,0:T(8,128)S(1)} %get-tuple-element.39.refs_2_, ...), custom_call_target="tpu_custom_call" | custom-call | flops 20000000 | bytes 5000000 | tf_op jit(solution)/shard_map/stencils/pallas_call | solution.py:216
  (96 shorter events, 34.9 us)
Async XLA Ops:
  3.3 26.3 %collective-permute-start = (f32[5,8,1440]{2,1,0:T(8,128)S(1)}, f32[5,8,1440]{2,1,0:T(8,128)S(1)}, u32[]{:S(2)}, u32[]{:S(2)}) collective-permute-start(f32[5,8,1440]{2,1,0:T(8,128)S(1)} %pad_maximum_fusion.4.refs_0_), channel_id=1, source_target_pairs={{0,4},{1,5},{2,6},{3,7},{4,0},{5,1},{6,2},{7,3},{8,12},{9,13},{10,... | collective-permute-start | bytes 691208 | tf_op jit(solution)/shard_map/ppermute | solution.py:21
  7.0 22.6 %collective-permute-start.4 = (f32[5,8,1440]{2,1,0:T(8,128)S(1)}, f32[5,8,1440]{2,1,0:T(8,128)S(1)}, u32[]{:S(2)}, u32[]{:S(2)}) collective-permute-start(f32[5,8,1440]{2,1,0:T(8,128)S(1)} %pad_maximum_fusion.5.refs_0_), channel_id=1, source_target_pairs={{0,1},{1,0},{2,3},{3,2},{4,5},{5,4},{6,7},{7,6},{8,9},{9,8},{10,11... | collective-permute-start | bytes 691208 | tf_op jit(solution)/shard_map/ppermute | solution.py:21
  7.3 32.9 %collective-permute-start.3 = (f32[5,8,1440]{2,1,0:T(8,128)S(1)}, f32[5,8,1440]{2,1,0:T(8,128)S(1)}, u32[]{:S(2)}, u32[]{:S(2)}) collective-permute-start(f32[5,8,1440]{2,1,0:T(8,128)S(1)} %pad_maximum_fusion.5.refs_0_), channel_id=1, source_target_pairs={{0,4},{1,5},{2,6},{3,7},{4,0},{5,1},{6,2},{7,3},{8,12},{9,13},{10,... | collective-permute-start | bytes 691208 | tf_op jit(solution)/shard_map/ppermute | solution.py:21
  7.6 32.6 %collective-permute-start.7 = (f32[5,8,1440]{2,1,0:T(8,128)S(1)}, f32[5,8,1440]{2,1,0:T(8,128)S(1)}, u32[]{:S(2)}, u32[]{:S(2)}) collective-permute-start(f32[5,8,1440]{2,1,0:T(8,128)S(1)} %pad_maximum_fusion.6.refs_0_), channel_id=1, source_target_pairs={{0,1},{1,0},{2,3},{3,2},{4,5},{5,4},{6,7},{7,6},{8,9},{9,8},{10,11... | collective-permute-start | bytes 691208 | tf_op jit(solution)/shard_map/ppermute | solution.py:21
  10.8 34.7 %collective-permute-start.6 = (f32[5,8,1440]{2,1,0:T(8,128)S(1)}, f32[5,8,1440]{2,1,0:T(8,128)S(1)}, u32[]{:S(2)}, u32[]{:S(2)}) collective-permute-start(f32[5,8,1440]{2,1,0:T(8,128)S(1)} %pad_maximum_fusion.6.refs_0_), channel_id=1, source_target_pairs={{0,4},{1,5},{2,6},{3,7},{4,0},{5,1},{6,2},{7,3},{8,12},{9,13},{10,... | collective-permute-start | bytes 691208 | tf_op jit(solution)/shard_map/ppermute | solution.py:21
  29.6 20.8 %collective-permute-start.9 = (f32[5,8,1440]{2,1,0:T(8,128)S(1)}, f32[5,8,1440]{2,1,0:T(8,128)S(1)}, u32[]{:S(2)}, u32[]{:S(2)}) collective-permute-start(f32[5,8,1440]{2,1,0:T(8,128)S(1)} %pad_maximum_fusion.7.refs_0_), channel_id=1, source_target_pairs={{0,4},{1,5},{2,6},{3,7},{4,0},{5,1},{6,2},{7,3},{8,12},{9,13},{10,... | collective-permute-start | bytes 691208 | tf_op jit(solution)/shard_map/ppermute | solution.py:21
  29.7 20.8 %collective-permute-start.2 = (f32[5,8,1440]{2,1,0:T(8,128)S(1)}, f32[5,8,1440]{2,1,0:T(8,128)S(1)}, u32[]{:S(2)}, u32[]{:S(2)}) collective-permute-start(f32[5,8,1440]{2,1,0:T(8,128)S(1)} %collective-permute-done.refs_1_), channel_id=1, source_target_pairs={{0,1},{1,0},{2,3},{3,2},{4,5},{5,4},{6,7},{7,6},{8,9},{9,8},{10,11... | collective-permute-start | bytes 691208 | tf_op jit(solution)/shard_map/ppermute | solution.py:21
  40.1 13.8 %collective-permute-start.5 = (f32[5,8,1440]{2,1,0:T(8,128)S(1)}, f32[5,8,1440]{2,1,0:T(8,128)S(1)}, u32[]{:S(2)}, u32[]{:S(2)}) collective-permute-start(f32[5,8,1440]{2,1,0:T(8,128)S(1)} %collective-permute-done.3.refs_1_), channel_id=1, source_target_pairs={{0,1},{1,0},{2,3},{3,2},{4,5},{5,4},{6,7},{7,6},{8,9},{9,8},{10,11... | collective-permute-start | bytes 691208 | tf_op jit(solution)/shard_map/ppermute | solution.py:21
  40.2 24.5 %collective-permute-start.10 = (f32[5,8,1440]{2,1,0:T(8,128)S(1)}, f32[5,8,1440]{2,1,0:T(8,128)S(1)}, u32[]{:S(2)}, u32[]{:S(2)}) collective-permute-start(f32[5,8,1440]{2,1,0:T(8,128)S(1)} %pad_maximum_fusion.7.refs_0_), channel_id=1, source_target_pairs={{0,1},{1,0},{2,3},{3,2},{4,5},{5,4},{6,7},{7,6},{8,9},{9,8},{10,11... | collective-permute-start | bytes 691208 | tf_op jit(solution)/shard_map/ppermute | solution.py:21
  45.4 13.9 %collective-permute-start.8 = (f32[5,8,1440]{2,1,0:T(8,128)S(1)}, f32[5,8,1440]{2,1,0:T(8,128)S(1)}, u32[]{:S(2)}, u32[]{:S(2)}) collective-permute-start(f32[5,8,1440]{2,1,0:T(8,128)S(1)} %collective-permute-done.6.refs_1_), channel_id=1, source_target_pairs={{0,1},{1,0},{2,3},{3,2},{4,5},{5,4},{6,7},{7,6},{8,9},{9,8},{10,11... | collective-permute-start | bytes 691208 | tf_op jit(solution)/shard_map/ppermute | solution.py:21
  50.4 14.3 %collective-permute-start.11 = (f32[5,8,1440]{2,1,0:T(8,128)S(1)}, f32[5,8,1440]{2,1,0:T(8,128)S(1)}, u32[]{:S(2)}, u32[]{:S(2)}) collective-permute-start(f32[5,8,1440]{2,1,0:T(8,128)S(1)} %collective-permute-done.9.refs_1_), channel_id=1, source_target_pairs={{0,1},{1,0},{2,3},{3,2},{4,5},{5,4},{6,7},{7,6},{8,9},{9,8},{10,11... | collective-permute-start | bytes 691208 | tf_op jit(solution)/shard_map/ppermute | solution.py:21
  50.5 19.5 %collective-permute-start.18 = (f32[4,3,1440]{2,1,0:T(4,128)}, f32[4,3,1440]{2,1,0:T(4,128)S(1)}, u32[]{:S(2)}, u32[]{:S(2)}) collective-permute-start(f32[4,3,1440]{2,1,0:T(4,128)} %get-tuple-element.56), channel_id=1, source_target_pairs={{0,8},{8,16},{16,24},{1,9},{9,17},{17,25},{2,10},{10,18},{18,26},{... | collective-permute-start | bytes 207368 | tf_op jit(solution)/shard_map/ppermute | solution.py:29
  54.0 19.1 %collective-permute-start.19 = (f32[4,3,1440]{2,1,0:T(4,128)}, f32[4,3,1440]{2,1,0:T(4,128)}, u32[]{:S(2)}, u32[]{:S(2)}) collective-permute-start(f32[4,3,1440]{2,1,0:T(4,128)} %get-tuple-element.57), channel_id=1, source_target_pairs={{8,0},{16,8},{24,16},{9,1},{17,9},{25,17},{10,2},{18,10},{26,18},{... | collective-permute-start | bytes 207368 | tf_op jit(solution)/shard_map/ppermute | solution.py:30
  69.9 14.5 %collective-permute-start.14 = (f32[5,8,1536]{2,1,0:T(8,128)S(1)}, f32[5,8,1536]{2,1,0:T(8,128)S(1)}, u32[]{:S(2)}, u32[]{:S(2)}) collective-permute-start(f32[5,8,1536]{2,1,0:T(8,128)S(1)} %get-tuple-element.32), channel_id=1, source_target_pairs={{0,2},{1,3},{2,0},{3,1},{4,6},{5,7},{6,4},{7,5},{8,10},{9,11},{10,... | collective-permute-start | bytes 737288 | tf_op jit(solution)/shard_map/ppermute | solution.py:21
  69.9 17.3 %collective-permute-start.15 = (f32[5,8,1536]{2,1,0:T(8,128)S(1)}, f32[5,8,1536]{2,1,0:T(8,128)S(1)}, u32[]{:S(2)}, u32[]{:S(2)}) collective-permute-start(f32[5,8,1536]{2,1,0:T(8,128)S(1)} %get-tuple-element.33), channel_id=1, source_target_pairs={{0,2},{1,3},{2,0},{3,1},{4,6},{5,7},{6,4},{7,5},{8,10},{9,11},{10,... | collective-permute-start | bytes 737288 | tf_op jit(solution)/shard_map/ppermute | solution.py:21
  107.9 31.6 %collective-permute-start.20 = (f32[5,8,1440]{2,1,0:T(8,128)S(1)}, f32[5,8,1440]{2,1,0:T(8,128)S(1)}, u32[]{:S(2)}, u32[]{:S(2)}) collective-permute-start(f32[5,8,1440]{2,1,0:T(8,128)S(1)} %get-tuple-element.34.refs_0_), channel_id=1, source_target_pairs={{0,4},{1,5},{2,6},{3,7},{4,0},{5,1},{6,2},{7,3},{8,12},{9,13},{10,... | collective-permute-start | bytes 691208 | tf_op jit(solution)/shard_map/ppermute | solution.py:21
  111.7 33.0 %collective-permute-start.23 = (f32[5,8,1440]{2,1,0:T(8,128)S(1)}, f32[5,8,1440]{2,1,0:T(8,128)S(1)}, u32[]{:S(2)}, u32[]{:S(2)}) collective-permute-start(f32[5,8,1440]{2,1,0:T(8,128)S(1)} %get-tuple-element.36.refs_0_), channel_id=1, source_target_pairs={{0,4},{1,5},{2,6},{3,7},{4,0},{5,1},{6,2},{7,3},{8,12},{9,13},{10,... | collective-permute-start | bytes 691208 | tf_op jit(solution)/shard_map/ppermute | solution.py:21
  111.8 33.0 %collective-permute-start.24 = (f32[5,8,1440]{2,1,0:T(8,128)S(1)}, f32[5,8,1440]{2,1,0:T(8,128)S(1)}, u32[]{:S(2)}, u32[]{:S(2)}) collective-permute-start(f32[5,8,1440]{2,1,0:T(8,128)S(1)} %get-tuple-element.36.refs_0_), channel_id=1, source_target_pairs={{0,1},{1,0},{2,3},{3,2},{4,5},{5,4},{6,7},{7,6},{8,9},{9,8},{10,11... | collective-permute-start | bytes 691208 | tf_op jit(solution)/shard_map/ppermute | solution.py:21
  111.9 38.2 %collective-permute-start.26 = (f32[5,8,1440]{2,1,0:T(8,128)S(1)}, f32[5,8,1440]{2,1,0:T(8,128)S(1)}, u32[]{:S(2)}, u32[]{:S(2)}) collective-permute-start(f32[5,8,1440]{2,1,0:T(8,128)S(1)} %get-tuple-element.38.refs_0_), channel_id=1, source_target_pairs={{0,4},{1,5},{2,6},{3,7},{4,0},{5,1},{6,2},{7,3},{8,12},{9,13},{10,... | collective-permute-start | bytes 691208 | tf_op jit(solution)/shard_map/ppermute | solution.py:21
  114.7 40.4 %collective-permute-start.29 = (f32[5,8,1440]{2,1,0:T(8,128)S(1)}, f32[5,8,1440]{2,1,0:T(8,128)S(1)}, u32[]{:S(2)}, u32[]{:S(2)}) collective-permute-start(f32[5,8,1440]{2,1,0:T(8,128)S(1)} %get-tuple-element.40.refs_0_), channel_id=1, source_target_pairs={{0,4},{1,5},{2,6},{3,7},{4,0},{5,1},{6,2},{7,3},{8,12},{9,13},{10,... | collective-permute-start | bytes 691208 | tf_op jit(solution)/shard_map/ppermute | solution.py:21
  139.5 15.6 %collective-permute-start.22 = (f32[5,8,1440]{2,1,0:T(8,128)S(1)}, f32[5,8,1440]{2,1,0:T(8,128)S(1)}, u32[]{:S(2)}, u32[]{:S(2)}) collective-permute-start(f32[5,8,1440]{2,1,0:T(8,128)S(1)} %collective-permute-done.20.refs_1_), channel_id=1, source_target_pairs={{0,1},{1,0},{2,3},{3,2},{4,5},{5,4},{6,7},{7,6},{8,9},{9,8},{10,11... | collective-permute-start | bytes 691208 | tf_op jit(solution)/shard_map/ppermute | solution.py:21
  144.8 14.9 %collective-permute-start.27 = (f32[5,8,1440]{2,1,0:T(8,128)S(1)}, f32[5,8,1440]{2,1,0:T(8,128)S(1)}, u32[]{:S(2)}, u32[]{:S(2)}) collective-permute-start(f32[5,8,1440]{2,1,0:T(8,128)S(1)} %get-tuple-element.38.refs_0_), channel_id=1, source_target_pairs={{0,1},{1,0},{2,3},{3,2},{4,5},{5,4},{6,7},{7,6},{8,9},{9,8},{10,11... | collective-permute-start | bytes 691208 | tf_op jit(solution)/shard_map/ppermute | solution.py:21
  163.7 13.3 %collective-permute-start.34 = (f32[5,8,1536]{2,1,0:T(8,128)S(1)}, f32[5,8,1536]{2,1,0:T(8,128)S(1)}, u32[]{:S(2)}, u32[]{:S(2)}) collective-permute-start(f32[5,8,1536]{2,1,0:T(8,128)S(1)} %get-tuple-element.44), channel_id=1, source_target_pairs={{0,2},{1,3},{2,0},{3,1},{4,6},{5,7},{6,4},{7,5},{8,10},{9,11},{10,... | collective-permute-start | bytes 737288 | tf_op jit(solution)/shard_map/ppermute | solution.py:21
  165.8 15.5 %collective-permute-start.35 = (f32[5,8,1536]{2,1,0:T(8,128)S(1)}, f32[5,8,1536]{2,1,0:T(8,128)S(1)}, u32[]{:S(2)}, u32[]{:S(2)}) collective-permute-start(f32[5,8,1536]{2,1,0:T(8,128)S(1)} %get-tuple-element.45), channel_id=1, source_target_pairs={{0,2},{1,3},{2,0},{3,1},{4,6},{5,7},{6,4},{7,5},{8,10},{9,11},{10,... | collective-permute-start | bytes 737288 | tf_op jit(solution)/shard_map/ppermute | solution.py:21
  (18 other events, 121.7 us)

commit v4 on v3

--- a/solution.py
+++ b/solution.py
@@ -271,20 +271,38 @@
     fields = [
         jnp.concatenate([air_mass[None, l], tracer_mass[:, l]], axis=0) for l in range(levels)
     ]
-    for step in range(ITERS):
-        held = [[f] for f in fields]
-        stride = 4
-        while stride < count:
-            for l in range(levels):
-                held[l] = held[l] + [exchange(x, stride) for x in held[l]]
-            stride *= 2
+    def finish(group, call, held):
         mine, theirs = [], []
-        for l in range(levels):
+        for l in group:
             other = [exchange(x, 1) for x in held[l]]
             kept, sent = cut_windows(held[l], other, plan[l])
             mine.append(kept)
             theirs.append(exchange(sent, 2))
-        fields = stencils(mine, theirs, frac, courant, width, step)
+        rows = slice(group[0], group[-1] + 1)
+        done = stencils(mine, theirs, frac[rows], courant[rows], width, call)
+        for l, value in zip(group, done):
+            fields[l] = value
+
+    groups = [range(0, levels // 2), range(levels // 2, levels)]
+    arrived = None
+    for step in range(ITERS):
+        for g, group in enumerate(groups):
+            held = {l: [fields[l]] for l in group}
+            if arrived is not None:
+                arrived, held = lax.optimization_barrier((arrived, held))
+                for l in previous:
+                    waiting[l] = arrived[l]
+            stride = 4
+            while stride < count:
+                for l in group:
+                    held[l] = held[l] + [exchange(x, stride) for x in held[l]]
+                stride *= 2
+            if arrived is not None:
+                finish(previous, previous_id, waiting)
+            previous, previous_id = group, step * len(groups) + g
+            waiting = dict(held)
+            arrived = dict(held)
+    finish(previous, previous_id, waiting)
     result = jnp.stack(fields, axis=1)
     return (result[0], result[1:])
 

time: 203 us -> 171 us (0.84)
  waiting for transfers between devices: 104 us -> 64.8 us
  starting transfers between devices: 32.9 us -> 39.1 us
  Pallas kernels: 56 us -> 61 us
  local copies, waits for them, and re-layouts: 7.06 us -> 4.06 us
    ppermute x32, waiting for transfers between devices: 103 us -> 62.4 us  [exchange(): return lax.ppermute(array, 'lon', [(i, i ^ stride) for i in range(count)])]
    ppermute x32, starting transfers between devices: 24.7 us -> 30.7 us  [exchange(): return lax.ppermute(array, 'lon', [(i, i ^ stride) for i in range(count)])]
    pallas_call x2 -> x4, Pallas kernels: 40.2 us -> 45.2 us  [stencils(): pl.pallas_call(functools.partial(stencil_kernel, levels, rows), out_shape...]
  transfers between devices with their start and end apart: 36 -> 36, of which waited for: 15 -> 12; matrix products, arithmetic and copies ran while one was open for 2% -> 0% of each run, Pallas kernels for 8% -> 29%
where the time goes in v4:
time: 171 us
  waiting for transfers between devices  64.8 us (38%)
  Pallas kernels  61 us (36%)
  starting transfers between devices  39.1 us (23%)
  local copies, waits for them, and re-layouts  4.06 us (2%)
    ppermute x32, waiting for transfers between devices, exchange(): return lax.ppermute(array, 'lon', [(i, i ^ stride) for i in range(count)])  62.4 us
    pallas_call x4, Pallas kernels, stencils(): pl.pallas_call(functools.partial(stencil_kernel, levels, rows), out_shape...  45.2 us
    ppermute x32, starting transfers between devices, exchange(): return lax.ppermute(array, 'lon', [(i, i ^ stride) for i in range(count)])  30.7 us
    pallas_call x8, Pallas kernels, cut_windows(): pl.pallas_call(functools.partial(window_kernel, held, lead, width), out_s...  15.8 us
    ppermute x1, starting transfers between devices, local(): lax.ppermute(zonal_frac[..., :HALO], 'lon', [(b, a) for a, b in ring])  3.54 us
    ppermute x1, starting transfers between devices, lat_halos(): lax.ppermute(lax.slice_in_dim(block, size - HALO, size, axis=dim), 'lat',...  3.53 us
  transfers between devices with their start and end apart: 36, of which 12 were waited for; matrix products, arithmetic and copies ran while one was open for 0% of the time, Pallas kernels for 29%

profile of v4, /device:TPU:0, one launch (start us, length us, event | category | flops | bytes accessed | tf_op | source)
XLA Modules:
  0.0 171.2 jit_solution(3486886812827761253)
XLA Ops:
  2.0 4.1 %collective-permute-start = (f32[5,8,1440]{2,1,0:T(8,128)S(1)}, f32[5,8,1440]{2,1,0:T(8,128)S(1)}, u32[]{:S(2)}, u32[]{:S(2)}) collective-permute-start(f32[5,8,1440]{2,1,0:T(8,128)S(1)} %pad_maximum_fusion.4.refs_0_), channel_id=1, source_target_pairs={{0,4},{1,5},{2,6},{3,7},{4,0},{5,1},{6,2},{7,3},{8,12},{9,13},{10,... | collective-permute-start | bytes 691208 | tf_op jit(solution)/shard_map/ppermute | solution.py:21
  7.2 3.5 %collective-permute-start.12 = (f32[4,3,1440]{2,1,0:T(4,128)S(1)}, f32[4,3,1440]{2,1,0:T(4,128)S(1)}, u32[]{:S(2)}, u32[]{:S(2)}) collective-permute-start(f32[4,3,1440]{2,1,0:T(4,128)S(1)} %get-tuple-element.96), channel_id=1, source_target_pairs={{0,8},{8,16},{16,24},{1,9},{9,17},{17,25},{2,10},{10,18},{18,26},{... | collective-permute-start | bytes 207368 | tf_op jit(solution)/shard_map/ppermute | solution.py:29
  10.8 3.5 %collective-permute-start.11 = (f32[4,8,3]{2,1,0:T(8,128)S(1)}, f32[4,8,3]{2,1,0:T(8,128)S(1)}, u32[]{:S(2)}, u32[]{:S(2)}) collective-permute-start(f32[4,8,3]{2,1,0:T(8,128)S(1)} %get-tuple-element.98), channel_id=1, source_target_pairs={{1,0},{2,1},{3,2},{4,3},{5,4},{6,5},{7,6},{0,7},{9,8},{10,9},{11,1... | collective-permute-start | bytes 1160 | tf_op jit(solution)/shard_map/ppermute | solution.py:264
  15.3 2.4 %collective-permute-done.10 = f32[4,8,3]{2,1,0:T(8,128)S(1)} collective-permute-done((f32[4,8,3]{2,1,0:T(8,128)S(1)}, f32[4,8,3]{2,1,0:T(8,128)S(1)}, u32[]{:S(2)}, u32[]{:S(2)}) %collective-permute-start.10) | collective-permute-done | bytes 416 | tf_op jit(solution)/shard_map/ppermute | solution.py:263
  19.2 4.4 %collective-permute-done.refs_1_ = f32[5,8,1440]{2,1,0:T(8,128)S(1)} collective-permute-done((f32[5,8,1440]{2,1,0:T(8,128)S(1)}, f32[5,8,1440]{2,1,0:T(8,128)S(1)}, u32[]{:S(2)}, u32[]{:S(2)}) %collective-permute-start) | collective-permute-done | bytes 230432 | tf_op jit(solution)/shard_map/ppermute | solution.py:21
  23.6 4.4 %collective-permute-done.1.refs_1_ = f32[5,8,1440]{2,1,0:T(8,128)S(1)} collective-permute-done((f32[5,8,1440]{2,1,0:T(8,128)S(1)}, f32[5,8,1440]{2,1,0:T(8,128)S(1)}, u32[]{:S(2)}, u32[]{:S(2)}) %collective-permute-start.1) | collective-permute-done | bytes 230432 | tf_op jit(solution)/shard_map/ppermute | solution.py:21
  29.1 8.3 %collective-permute-start.2 = (f32[5,8,1440]{2,1,0:T(8,128)S(1)}, f32[5,8,1440]{2,1,0:T(8,128)S(1)}, u32[]{:S(2)}, u32[]{:S(2)}) collective-permute-start(f32[5,8,1440]{2,1,0:T(8,128)S(1)} %get-tuple-element.58.refs_0_), channel_id=1, source_target_pairs={{0,4},{1,5},{2,6},{3,7},{4,0},{5,1},{6,2},{7,3},{8,12},{9,13},{10,... | collective-permute-start | bytes 691208 | tf_op jit(solution)/shard_map/ppermute | solution.py:21
  41.6 2.1 %collective-permute-start.8 = (f32[5,8,1536]{2,1,0:T(8,128)S(1)}, f32[5,8,1536]{2,1,0:T(8,128)S(1)}, u32[]{:S(2)}, u32[]{:S(2)}) collective-permute-start(f32[5,8,1536]{2,1,0:T(8,128)S(1)} %get-tuple-element.52), channel_id=1, source_target_pairs={{0,2},{1,3},{2,0},{3,1},{4,6},{5,7},{6,4},{7,5},{8,10},{9,11},{10,... | collective-permute-start | bytes 737288 | tf_op jit(solution)/shard_map/ppermute | solution.py:21
  43.7 14.1 %collective-permute-done.9.refs_3_ = f32[5,8,1536]{2,1,0:T(8,128)S(1)} collective-permute-done((f32[5,8,1536]{2,1,0:T(8,128)S(1)}, f32[5,8,1536]{2,1,0:T(8,128)S(1)}, u32[]{:S(2)}, u32[]{:S(2)}) %collective-permute-start.9) | collective-permute-done | bytes 245792 | tf_op jit(solution)/shard_map/ppermute | solution.py:21
  57.9 2.8 %collective-permute-done.8.refs_2_ = f32[5,8,1536]{2,1,0:T(8,128)S(1)} collective-permute-done((f32[5,8,1536]{2,1,0:T(8,128)S(1)}, f32[5,8,1536]{2,1,0:T(8,128)S(1)}, u32[]{:S(2)}, u32[]{:S(2)}) %collective-permute-start.8) | collective-permute-done | bytes 245792 | tf_op jit(solution)/shard_map/ppermute | solution.py:21
  60.7 11.2 %stencils.4 = (f32[5,8,1440]{2,1,0:T(8,128)S(1)}, f32[5,8,1440]{2,1,0:T(8,128)S(1)}) custom-call(f32[5,8,1536]{2,1,0:T(8,128)S(1)} %get-tuple-element.48.refs_0_, f32[5,8,1536]{2,1,0:T(8,128)S(1)} %get-tuple-element.51.refs_1_, f32[5,8,1536]{2,1,0:T(8,128)S(1)} %collective-permute-done.8.refs_2_, f32[5,8,1536]{2,1,0:T(8,128)S(1)} %collective-permute-done.9.refs_3_, ...), custom_call_target="tpu_custom_call" | custom-call | flops 20000000 | bytes 5000000 | tf_op jit(solution)/shard_map/stencils/pallas_call | solution.py:216
  77.9 2.1 %collective-permute-start.20 = (f32[5,8,1536]{2,1,0:T(8,128)S(1)}, f32[5,8,1536]{2,1,0:T(8,128)S(1)}, u32[]{:S(2)}, u32[]{:S(2)}) collective-permute-start(f32[5,8,1536]{2,1,0:T(8,128)S(1)} %get-tuple-element.64), channel_id=1, source_target_pairs={{0,2},{1,3},{2,0},{3,1},{4,6},{5,7},{6,4},{7,5},{8,10},{9,11},{10,... | collective-permute-start | bytes 737288 | tf_op jit(solution)/shard_map/ppermute | solution.py:21
  80.0 2.9 %collective-permute-start.15 = (f32[5,8,1440]{2,1,0:T(8,128)S(1)}, f32[5,8,1440]{2,1,0:T(8,128)S(1)}, u32[]{:S(2)}, u32[]{:S(2)}) collective-permute-start(f32[5,8,1440]{2,1,0:T(8,128)S(1)} %get-tuple-element.71.refs_0_), channel_id=1, source_target_pairs={{0,4},{1,5},{2,6},{3,7},{4,0},{5,1},{6,2},{7,3},{8,12},{9,13},{10,... | collective-permute-start | bytes 691208 | tf_op jit(solution)/shard_map/ppermute | solution.py:21
  82.9 6.7 %collective-permute-done.21.refs_3_ = f32[5,8,1536]{2,1,0:T(8,128)S(1)} collective-permute-done((f32[5,8,1536]{2,1,0:T(8,128)S(1)}, f32[5,8,1536]{2,1,0:T(8,128)S(1)}, u32[]{:S(2)}, u32[]{:S(2)}) %collective-permute-start.21) | collective-permute-done | bytes 245792 | tf_op jit(solution)/shard_map/ppermute | solution.py:21
  89.6 4.5 %collective-permute-done.20.refs_2_ = f32[5,8,1536]{2,1,0:T(8,128)S(1)} collective-permute-done((f32[5,8,1536]{2,1,0:T(8,128)S(1)}, f32[5,8,1536]{2,1,0:T(8,128)S(1)}, u32[]{:S(2)}, u32[]{:S(2)}) %collective-permute-start.20) | collective-permute-done | bytes 245792 | tf_op jit(solution)/shard_map/ppermute | solution.py:21
  94.1 11.4 %stencils.5 = (f32[5,8,1440]{2,1,0:T(8,128)S(1)}, f32[5,8,1440]{2,1,0:T(8,128)S(1)}) custom-call(f32[5,8,1536]{2,1,0:T(8,128)S(1)} %get-tuple-element.60.refs_0_, f32[5,8,1536]{2,1,0:T(8,128)S(1)} %get-tuple-element.63.refs_1_, f32[5,8,1536]{2,1,0:T(8,128)S(1)} %collective-permute-done.20.refs_2_, f32[5,8,1536]{2,1,0:T(8,128)S(1)} %collective-permute-done.21.refs_3_, ...), custom_call_target="tpu_custom_call" | custom-call | flops 20000000 | bytes 5000000 | tf_op jit(solution)/shard_map/stencils/pallas_call | solution.py:216
  107.0 2.0 %collective-permute-start.28 = (f32[5,8,1440]{2,1,0:T(8,128)S(1)}, f32[5,8,1440]{2,1,0:T(8,128)S(1)}, u32[]{:S(2)}, u32[]{:S(2)}) collective-permute-start(f32[5,8,1440]{2,1,0:T(8,128)S(1)} %get-tuple-element.78.refs_0_), channel_id=1, source_target_pairs={{0,4},{1,5},{2,6},{3,7},{4,0},{5,1},{6,2},{7,3},{8,12},{9,13},{10,... | collective-permute-start | bytes 691208 | tf_op jit(solution)/shard_map/ppermute | solution.py:21
  109.5 16.2 %collective-permute-done.31.refs_1_ = f32[5,8,1440]{2,1,0:T(8,128)S(1)} collective-permute-done((f32[5,8,1440]{2,1,0:T(8,128)S(1)}, f32[5,8,1440]{2,1,0:T(8,128)S(1)}, u32[]{:S(2)}, u32[]{:S(2)}) %collective-permute-start.31) | collective-permute-done | bytes 230432 | tf_op jit(solution)/shard_map/ppermute | solution.py:21
  126.3 4.4 %collective-permute-done.28.refs_1_ = f32[5,8,1440]{2,1,0:T(8,128)S(1)} collective-permute-done((f32[5,8,1440]{2,1,0:T(8,128)S(1)}, f32[5,8,1440]{2,1,0:T(8,128)S(1)}, u32[]{:S(2)}, u32[]{:S(2)}) %collective-permute-start.28) | collective-permute-done | bytes 230432 | tf_op jit(solution)/shard_map/ppermute | solution.py:21
  134.8 2.1 %collective-permute-start.26 = (f32[5,8,1536]{2,1,0:T(8,128)S(1)}, f32[5,8,1536]{2,1,0:T(8,128)S(1)}, u32[]{:S(2)}, u32[]{:S(2)}) collective-permute-start(f32[5,8,1536]{2,1,0:T(8,128)S(1)} %get-tuple-element.74), channel_id=1, source_target_pairs={{0,2},{1,3},{2,0},{3,1},{4,6},{5,7},{6,4},{7,5},{8,10},{9,11},{10,... | collective-permute-start | bytes 737288 | tf_op jit(solution)/shard_map/ppermute | solution.py:21
  140.9 2.1 %collective-permute-start.34 = (f32[5,8,1536]{2,1,0:T(8,128)S(1)}, f32[5,8,1536]{2,1,0:T(8,128)S(1)}, u32[]{:S(2)}, u32[]{:S(2)}) collective-permute-start(f32[5,8,1536]{2,1,0:T(8,128)S(1)} %get-tuple-element.82), channel_id=1, source_target_pairs={{0,2},{1,3},{2,0},{3,1},{4,6},{5,7},{6,4},{7,5},{8,10},{9,11},{10,... | collective-permute-start | bytes 737288 | tf_op jit(solution)/shard_map/ppermute | solution.py:21
  143.0 3.8 %collective-permute-done.26.refs_2_ = f32[5,8,1536]{2,1,0:T(8,128)S(1)} collective-permute-done((f32[5,8,1536]{2,1,0:T(8,128)S(1)}, f32[5,8,1536]{2,1,0:T(8,128)S(1)}, u32[]{:S(2)}, u32[]{:S(2)}) %collective-permute-start.26) | collective-permute-done | bytes 245792 | tf_op jit(solution)/shard_map/ppermute | solution.py:21
  146.8 11.9 %stencils.6 = (f32[5,8,1440]{2,1,0:T(8,128)S(1)}, f32[5,8,1440]{2,1,0:T(8,128)S(1)}) custom-call(f32[5,8,1536]{2,1,0:T(8,128)S(1)} %get-tuple-element.70.refs_0_, f32[5,8,1536]{2,1,0:T(8,128)S(1)} %get-tuple-element.73.refs_1_, f32[5,8,1536]{2,1,0:T(8,128)S(1)} %collective-permute-done.26.refs_2_, f32[5,8,1536]{2,1,0:T(8,128)S(1)} %collective-permute-done.27.refs_3_, ...), custom_call_target="tpu_custom_call" | custom-call | flops 20000000 | bytes 5000000 | tf_op jit(solution)/shard_map/stencils/pallas_call | solution.py:216
  158.7 10.7 %stencils.7 = (f32[5,8,1440]{2,1,0:T(8,128)S(1)}, f32[5,8,1440]{2,1,0:T(8,128)S(1)}) custom-call(f32[5,8,1536]{2,1,0:T(8,128)S(1)} %get-tuple-element.79.refs_0_, f32[5,8,1536]{2,1,0:T(8,128)S(1)} %get-tuple-element.81.refs_1_, f32[5,8,1536]{2,1,0:T(8,128)S(1)} %collective-permute-done.34.refs_2_, f32[5,8,1536]{2,1,0:T(8,128)S(1)} %collective-permute-done.35.refs_3_, ...), custom_call_target="tpu_custom_call" | custom-call | flops 20000000 | bytes 5000000 | tf_op jit(solution)/shard_map/stencils/pallas_call | solution.py:216
  (95 shorter events, 28.3 us)
Async XLA Ops:
  2.0 21.6 %collective-permute-start = (f32[5,8,1440]{2,1,0:T(8,128)S(1)}, f32[5,8,1440]{2,1,0:T(8,128)S(1)}, u32[]{:S(2)}, u32[]{:S(2)}) collective-permute-start(f32[5,8,1440]{2,1,0:T(8,128)S(1)} %pad_maximum_fusion.4.refs_0_), channel_id=1, source_target_pairs={{0,4},{1,5},{2,6},{3,7},{4,0},{5,1},{6,2},{7,3},{8,12},{9,13},{10,... | collective-permute-start | bytes 691208 | tf_op jit(solution)/shard_map/ppermute | solution.py:21
  6.1 21.9 %collective-permute-start.1 = (f32[5,8,1440]{2,1,0:T(8,128)S(1)}, f32[5,8,1440]{2,1,0:T(8,128)S(1)}, u32[]{:S(2)}, u32[]{:S(2)}) collective-permute-start(f32[5,8,1440]{2,1,0:T(8,128)S(1)} %pad_maximum_fusion.5.refs_0_), channel_id=1, source_target_pairs={{0,4},{1,5},{2,6},{3,7},{4,0},{5,1},{6,2},{7,3},{8,12},{9,13},{10,... | collective-permute-start | bytes 691208 | tf_op jit(solution)/shard_map/ppermute | solution.py:21
  7.2 21.4 %collective-permute-start.12 = (f32[4,3,1440]{2,1,0:T(4,128)S(1)}, f32[4,3,1440]{2,1,0:T(4,128)S(1)}, u32[]{:S(2)}, u32[]{:S(2)}) collective-permute-start(f32[4,3,1440]{2,1,0:T(4,128)S(1)} %get-tuple-element.96), channel_id=1, source_target_pairs={{0,8},{8,16},{16,24},{1,9},{9,17},{17,25},{2,10},{10,18},{18,26},{... | collective-permute-start | bytes 207368 | tf_op jit(solution)/shard_map/ppermute | solution.py:29
  17.7 11.3 %collective-permute-start.13 = (f32[4,3,1440]{2,1,0:T(4,128)S(1)}, f32[4,3,1440]{2,1,0:T(4,128)S(1)}, u32[]{:S(2)}, u32[]{:S(2)}) collective-permute-start(f32[4,3,1440]{2,1,0:T(4,128)S(1)} %get-tuple-element.97), channel_id=1, source_target_pairs={{8,0},{16,8},{24,16},{9,1},{17,9},{25,17},{10,2},{18,10},{26,18},{... | collective-permute-start | bytes 207368 | tf_op jit(solution)/shard_map/ppermute | solution.py:30
  28.5 11.1 %collective-permute-start.4 = (f32[5,8,1440]{2,1,0:T(8,128)S(1)}, f32[5,8,1440]{2,1,0:T(8,128)S(1)}, u32[]{:S(2)}, u32[]{:S(2)}) collective-permute-start(f32[5,8,1440]{2,1,0:T(8,128)S(1)} %pad_maximum_fusion.4.refs_0_), channel_id=1, source_target_pairs={{0,1},{1,0},{2,3},{3,2},{4,5},{5,4},{6,7},{7,6},{8,9},{9,8},{10,11... | collective-permute-start | bytes 691208 | tf_op jit(solution)/shard_map/ppermute | solution.py:21
  28.6 11.1 %collective-permute-start.5 = (f32[5,8,1440]{2,1,0:T(8,128)S(1)}, f32[5,8,1440]{2,1,0:T(8,128)S(1)}, u32[]{:S(2)}, u32[]{:S(2)}) collective-permute-start(f32[5,8,1440]{2,1,0:T(8,128)S(1)} %collective-permute-done.refs_1_), channel_id=1, source_target_pairs={{0,1},{1,0},{2,3},{3,2},{4,5},{5,4},{6,7},{7,6},{8,9},{9,8},{10,11... | collective-permute-start | bytes 691208 | tf_op jit(solution)/shard_map/ppermute | solution.py:21
  29.1 42.8 %collective-permute-start.2 = (f32[5,8,1440]{2,1,0:T(8,128)S(1)}, f32[5,8,1440]{2,1,0:T(8,128)S(1)}, u32[]{:S(2)}, u32[]{:S(2)}) collective-permute-start(f32[5,8,1440]{2,1,0:T(8,128)S(1)} %get-tuple-element.58.refs_0_), channel_id=1, source_target_pairs={{0,4},{1,5},{2,6},{3,7},{4,0},{5,1},{6,2},{7,3},{8,12},{9,13},{10,... | collective-permute-start | bytes 691208 | tf_op jit(solution)/shard_map/ppermute | solution.py:21
  37.5 34.4 %collective-permute-start.3 = (f32[5,8,1440]{2,1,0:T(8,128)S(1)}, f32[5,8,1440]{2,1,0:T(8,128)S(1)}, u32[]{:S(2)}, u32[]{:S(2)}) collective-permute-start(f32[5,8,1440]{2,1,0:T(8,128)S(1)} %get-tuple-element.61.refs_0_), channel_id=1, source_target_pairs={{0,4},{1,5},{2,6},{3,7},{4,0},{5,1},{6,2},{7,3},{8,12},{9,13},{10,... | collective-permute-start | bytes 691208 | tf_op jit(solution)/shard_map/ppermute | solution.py:21
  39.6 18.3 %collective-permute-start.9 = (f32[5,8,1536]{2,1,0:T(8,128)S(1)}, f32[5,8,1536]{2,1,0:T(8,128)S(1)}, u32[]{:S(2)}, u32[]{:S(2)}) collective-permute-start(f32[5,8,1536]{2,1,0:T(8,128)S(1)} %get-tuple-element.53), channel_id=1, source_target_pairs={{0,2},{1,3},{2,0},{3,1},{4,6},{5,7},{6,4},{7,5},{8,10},{9,11},{10,... | collective-permute-start | bytes 737288 | tf_op jit(solution)/shard_map/ppermute | solution.py:21
  41.6 19.1 %collective-permute-start.8 = (f32[5,8,1536]{2,1,0:T(8,128)S(1)}, f32[5,8,1536]{2,1,0:T(8,128)S(1)}, u32[]{:S(2)}, u32[]{:S(2)}) collective-permute-start(f32[5,8,1536]{2,1,0:T(8,128)S(1)} %get-tuple-element.52), channel_id=1, source_target_pairs={{0,2},{1,3},{2,0},{3,1},{4,6},{5,7},{6,4},{7,5},{8,10},{9,11},{10,... | collective-permute-start | bytes 737288 | tf_op jit(solution)/shard_map/ppermute | solution.py:21
  75.8 13.8 %collective-permute-start.21 = (f32[5,8,1536]{2,1,0:T(8,128)S(1)}, f32[5,8,1536]{2,1,0:T(8,128)S(1)}, u32[]{:S(2)}, u32[]{:S(2)}) collective-permute-start(f32[5,8,1536]{2,1,0:T(8,128)S(1)} %get-tuple-element.65), channel_id=1, source_target_pairs={{0,2},{1,3},{2,0},{3,1},{4,6},{5,7},{6,4},{7,5},{8,10},{9,11},{10,... | collective-permute-start | bytes 737288 | tf_op jit(solution)/shard_map/ppermute | solution.py:21
  77.9 16.2 %collective-permute-start.20 = (f32[5,8,1536]{2,1,0:T(8,128)S(1)}, f32[5,8,1536]{2,1,0:T(8,128)S(1)}, u32[]{:S(2)}, u32[]{:S(2)}) collective-permute-start(f32[5,8,1536]{2,1,0:T(8,128)S(1)} %get-tuple-element.64), channel_id=1, source_target_pairs={{0,2},{1,3},{2,0},{3,1},{4,6},{5,7},{6,4},{7,5},{8,10},{9,11},{10,... | collective-permute-start | bytes 737288 | tf_op jit(solution)/shard_map/ppermute | solution.py:21
  80.0 25.5 %collective-permute-start.14 = (f32[5,8,1440]{2,1,0:T(8,128)S(1)}, f32[5,8,1440]{2,1,0:T(8,128)S(1)}, u32[]{:S(2)}, u32[]{:S(2)}) collective-permute-start(f32[5,8,1440]{2,1,0:T(8,128)S(1)} %get-tuple-element.68.refs_0_), channel_id=1, source_target_pairs={{0,4},{1,5},{2,6},{3,7},{4,0},{5,1},{6,2},{7,3},{8,12},{9,13},{10,... | collective-permute-start | bytes 691208 | tf_op jit(solution)/shard_map/ppermute | solution.py:21
  80.0 25.5 %collective-permute-start.15 = (f32[5,8,1440]{2,1,0:T(8,128)S(1)}, f32[5,8,1440]{2,1,0:T(8,128)S(1)}, u32[]{:S(2)}, u32[]{:S(2)}) collective-permute-start(f32[5,8,1440]{2,1,0:T(8,128)S(1)} %get-tuple-element.71.refs_0_), channel_id=1, source_target_pairs={{0,4},{1,5},{2,6},{3,7},{4,0},{5,1},{6,2},{7,3},{8,12},{9,13},{10,... | collective-permute-start | bytes 691208 | tf_op jit(solution)/shard_map/ppermute | solution.py:21
  106.1 19.7 %collective-permute-start.31 = (f32[5,8,1440]{2,1,0:T(8,128)S(1)}, f32[5,8,1440]{2,1,0:T(8,128)S(1)}, u32[]{:S(2)}, u32[]{:S(2)}) collective-permute-start(f32[5,8,1440]{2,1,0:T(8,128)S(1)} %get-tuple-element.80.refs_0_), channel_id=1, source_target_pairs={{0,4},{1,5},{2,6},{3,7},{4,0},{5,1},{6,2},{7,3},{8,12},{9,13},{10,... | collective-permute-start | bytes 691208 | tf_op jit(solution)/shard_map/ppermute | solution.py:21
  107.0 18.7 %collective-permute-start.22 = (f32[5,8,1440]{2,1,0:T(8,128)S(1)}, f32[5,8,1440]{2,1,0:T(8,128)S(1)}, u32[]{:S(2)}, u32[]{:S(2)}) collective-permute-start(f32[5,8,1440]{2,1,0:T(8,128)S(1)} %get-tuple-element.68.refs_0_), channel_id=1, source_target_pairs={{0,1},{1,0},{2,3},{3,2},{4,5},{5,4},{6,7},{7,6},{8,9},{9,8},{10,11... | collective-permute-start | bytes 691208 | tf_op jit(solution)/shard_map/ppermute | solution.py:21
  107.0 23.7 %collective-permute-start.28 = (f32[5,8,1440]{2,1,0:T(8,128)S(1)}, f32[5,8,1440]{2,1,0:T(8,128)S(1)}, u32[]{:S(2)}, u32[]{:S(2)}) collective-permute-start(f32[5,8,1440]{2,1,0:T(8,128)S(1)} %get-tuple-element.78.refs_0_), channel_id=1, source_target_pairs={{0,4},{1,5},{2,6},{3,7},{4,0},{5,1},{6,2},{7,3},{8,12},{9,13},{10,... | collective-permute-start | bytes 691208 | tf_op jit(solution)/shard_map/ppermute | solution.py:21
  109.0 23.7 %collective-permute-start.23 = (f32[5,8,1440]{2,1,0:T(8,128)S(1)}, f32[5,8,1440]{2,1,0:T(8,128)S(1)}, u32[]{:S(2)}, u32[]{:S(2)}) collective-permute-start(f32[5,8,1440]{2,1,0:T(8,128)S(1)} %collective-permute-done.14.refs_1_), channel_id=1, source_target_pairs={{0,1},{1,0},{2,3},{3,2},{4,5},{5,4},{6,7},{7,6},{8,9},{9,8},{10,11... | collective-permute-start | bytes 691208 | tf_op jit(solution)/shard_map/ppermute | solution.py:21
  109.3 25.5 %collective-permute-start.32 = (f32[5,8,1440]{2,1,0:T(8,128)S(1)}, f32[5,8,1440]{2,1,0:T(8,128)S(1)}, u32[]{:S(2)}, u32[]{:S(2)}) collective-permute-start(f32[5,8,1440]{2,1,0:T(8,128)S(1)} %get-tuple-element.80.refs_0_), channel_id=1, source_target_pairs={{0,1},{1,0},{2,3},{3,2},{4,5},{5,4},{6,7},{7,6},{8,9},{9,8},{10,11... | collective-permute-start | bytes 691208 | tf_op jit(solution)/shard_map/ppermute | solution.py:21
  125.8 11.1 %collective-permute-start.33 = (f32[5,8,1440]{2,1,0:T(8,128)S(1)}, f32[5,8,1440]{2,1,0:T(8,128)S(1)}, u32[]{:S(2)}, u32[]{:S(2)}) collective-permute-start(f32[5,8,1440]{2,1,0:T(8,128)S(1)} %collective-permute-done.31.refs_1_), channel_id=1, source_target_pairs={{0,1},{1,0},{2,3},{3,2},{4,5},{5,4},{6,7},{7,6},{8,9},{9,8},{10,11... | collective-permute-start | bytes 691208 | tf_op jit(solution)/shard_map/ppermute | solution.py:21
  125.8 13.2 %collective-permute-start.29 = (f32[5,8,1440]{2,1,0:T(8,128)S(1)}, f32[5,8,1440]{2,1,0:T(8,128)S(1)}, u32[]{:S(2)}, u32[]{:S(2)}) collective-permute-start(f32[5,8,1440]{2,1,0:T(8,128)S(1)} %get-tuple-element.78.refs_0_), channel_id=1, source_target_pairs={{0,1},{1,0},{2,3},{3,2},{4,5},{5,4},{6,7},{7,6},{8,9},{9,8},{10,11... | collective-permute-start | bytes 691208 | tf_op jit(solution)/shard_map/ppermute | solution.py:21
  134.8 12.0 %collective-permute-start.26 = (f32[5,8,1536]{2,1,0:T(8,128)S(1)}, f32[5,8,1536]{2,1,0:T(8,128)S(1)}, u32[]{:S(2)}, u32[]{:S(2)}) collective-permute-start(f32[5,8,1536]{2,1,0:T(8,128)S(1)} %get-tuple-element.74), channel_id=1, source_target_pairs={{0,2},{1,3},{2,0},{3,1},{4,6},{5,7},{6,4},{7,5},{8,10},{9,11},{10,... | collective-permute-start | bytes 737288 | tf_op jit(solution)/shard_map/ppermute | solution.py:21
  138.8 19.9 %collective-permute-start.35 = (f32[5,8,1536]{2,1,0:T(8,128)S(1)}, f32[5,8,1536]{2,1,0:T(8,128)S(1)}, u32[]{:S(2)}, u32[]{:S(2)}) collective-permute-start(f32[5,8,1536]{2,1,0:T(8,128)S(1)} %get-tuple-element.83), channel_id=1, source_target_pairs={{0,2},{1,3},{2,0},{3,1},{4,6},{5,7},{6,4},{7,5},{8,10},{9,11},{10,... | collective-permute-start | bytes 737288 | tf_op jit(solution)/shard_map/ppermute | solution.py:21
  140.9 17.8 %collective-permute-start.34 = (f32[5,8,1536]{2,1,0:T(8,128)S(1)}, f32[5,8,1536]{2,1,0:T(8,128)S(1)}, u32[]{:S(2)}, u32[]{:S(2)}) collective-permute-start(f32[5,8,1536]{2,1,0:T(8,128)S(1)} %get-tuple-element.82), channel_id=1, source_target_pairs={{0,2},{1,3},{2,0},{3,1},{4,6},{5,7},{6,4},{7,5},{8,10},{9,11},{10,... | collective-permute-start | bytes 737288 | tf_op jit(solution)/shard_map/ppermute | solution.py:21
  (16 other events, 76.5 us)
